TPU v7x, 256 devices: a whole 4x4x8 slice. The times are simulated.
256 devices in a mesh: tm: 8 (over z_lo, core), height: 32 (over x, y, z_hi).
Axes of the slice: x: 4, y: 4, z: 8 (z_hi: 2, z_lo: 4; z = z_hi * 4 + z_lo), core: 2. Of those that a mesh axis runs over, the one named last changes fastest.
Arguments:
- clean_latents: bfloat16 [32, 128, 16, 3072], P('tm', 'height'), may hold values from -6 to 6
- gaussian_noise: bfloat16 [32, 128, 16, 3072], P('tm', 'height'), may hold values from -6 to 6
- text_states: bfloat16 [256, 3072], replicated, may hold values from -6 to 6
- queries: bfloat16 [32, 128, 16, 1536], P('tm', 'height'), may hold values from -40 to 40
- key_states: bfloat16 [32, 128, 16, 1536], P('tm', 'height'), may hold values from -8 to 8
- cotangent: bfloat16 [32, 128, 16, 1536], P('tm', 'height'), may hold values from -240 to 240
- text_keys: bfloat16 [256, 1536], replicated, may hold values from -6 to 6
- window_radii: int32 [12, 3], replicated, may hold values from 0 to 1
- timestep: int32 [1], replicated, may hold values from 200 to 799
- sketch_seed: int32 [1], replicated, may hold values from 0 to 65535
- down_image: bfloat16 [3072, 16], replicated, may hold values from -0.109375 to 0.109375
- up_image: bfloat16 [16, 1536], replicated, may hold values from -1.5 to 1.5
- down_text: bfloat16 [3072, 16], replicated, may hold values from -0.109375 to 0.109375
- up_text: bfloat16 [16, 1536], replicated, may hold values from -1.5 to 1.5
Outputs:
- value_grad: bfloat16 [32, 128, 16, 1536], P('tm', 'height')
- grad_sketch: float32 [16384], replicated
All inputs are finite; a program needn't handle non-finite values.
Results may differ from a plain program's by a relative error of at most 0.0075.
Values may be sent and summed in bfloat16 or wider, within the bound.
A program may use at most 128 MiB of HBM per device.

v0:
```python
import jax
import jax.numpy as jnp
from jax import lax
from jax.sharding import PartitionSpec as P

SKETCH = 16384
TW = 8


def padded_2(block, sides, width):
    for axis, dim in sides:
        count = lax.axis_size(axis)
        forward = [(i, i + 1) for i in range(count - 1)]
        backward = [(target, source) for source, target in forward]
        low = lax.ppermute(
            lax.slice_in_dim(block, block.shape[dim] - width, None, axis=dim), axis, forward
        )
        high = lax.ppermute(lax.slice_in_dim(block, 0, width, axis=dim), axis, backward)
        block = jnp.concatenate([low, block, high], axis=dim)
    return block


def shifted(array, axis, by):
    size = lax.axis_size(axis)
    pairs = [(i, i + by) for i in range(size) if 0 <= i + by < size]
    return lax.ppermute(array, axis, pairs)


def tile_rows(block, width):
    frame_count, row_count, col_count = (block.shape[0], block.shape[1], block.shape[2])
    rest = block.shape[3:]
    col_tiles = col_count // width
    shaped = block.reshape((frame_count, row_count, col_tiles, width) + rest)
    order = (2, 0, 1, 3) + tuple(range(4, 4 + len(rest)))
    return jnp.transpose(shaped, order).reshape((col_tiles, frame_count * row_count * width) + rest)


def region_rows(padded, width):
    col_count = padded.shape[2] - 2 * width
    views = [
        tile_rows(padded[:, :, shift_col * width : shift_col * width + col_count], width)
        for shift_col in range(3)
    ]
    return jnp.concatenate(views, axis=1)


def window_mask(
    radius, frame_tile, row_tile, frame_tiles, row_tiles, col_tiles, frame_count, row_count, width
):
    region = 27 * frame_count * row_count * width
    position = jnp.arange(region, dtype=jnp.int32)
    col_step = position // (9 * frame_count * row_count * width) - 1
    frame_step = position // (3 * row_count * width) % (3 * frame_count) // frame_count - 1
    row_step = position // width % (3 * row_count) // row_count - 1
    inside = (
        (jnp.abs(frame_step) <= radius[0])
        & (jnp.abs(row_step) <= radius[1])
        & (jnp.abs(col_step) <= radius[2])
    )
    inside = inside & (frame_tile + frame_step >= 0) & (frame_tile + frame_step < frame_tiles)
    inside = inside & (row_tile + row_step >= 0) & (row_tile + row_step < row_tiles)
    col_index = jnp.arange(col_tiles, dtype=jnp.int32)[:, None]
    return (
        inside[None, :]
        & (col_index + col_step[None, :] >= 0)
        & (col_index + col_step[None, :] < col_tiles)
    )


def forward_head(query_head, key_region, text_head, cot_head, allowed, score_scale):
    image_scores = (
        jnp.einsum("cqd,cld->cql", query_head, key_region, preferred_element_type=jnp.float32)
        * score_scale
    )
    image_scores = jnp.where(allowed[:, None, :], image_scores, -jnp.inf)
    text_scores = (
        jnp.einsum("cqd,td->cqt", query_head, text_head, preferred_element_type=jnp.float32)
        * score_scale
    )
    row_max = jnp.maximum(jnp.max(image_scores, axis=-1), jnp.max(text_scores, axis=-1))
    total = jnp.sum(jnp.exp(image_scores - row_max[..., None]), axis=-1) + jnp.sum(
        jnp.exp(text_scores - row_max[..., None]), axis=-1
    )
    log_total = row_max + jnp.log(total)
    text_probs = jnp.exp(text_scores - log_total[..., None]).astype(jnp.bfloat16)
    text_part = jnp.einsum("cqt,cqd->td", text_probs, cot_head, preferred_element_type=jnp.float32)
    return (image_scores, log_total, text_part)


def place_back(spread, frame_count, row_count, width):
    col_tiles, head_width = (spread.shape[0], spread.shape[2])
    shaped = spread.reshape(col_tiles, 3, 3 * frame_count, 3 * row_count, width, head_width)
    placed = jnp.zeros((3 * frame_count, 3 * row_count, col_tiles, width, head_width), jnp.float32)
    for shift_col in range(3):
        moved = jnp.transpose(shaped[:, shift_col], (1, 2, 0, 3, 4))
        moved = jnp.pad(moved, ((0, 0), (0, 0), (1, 1), (0, 0), (0, 0)))
        placed = placed + moved[:, :, 2 - shift_col : 2 - shift_col + col_tiles]
    return placed.reshape(3 * frame_count, 3 * row_count, col_tiles * width, head_width)


def sketch_signs(seed_value, rows, width):
    row_part = jnp.arange(rows, dtype=jnp.int32)[:, None] * width
    position = row_part + jnp.arange(width, dtype=jnp.int32)[None, :]
    mixed_bits = position * 1103515245 + seed_value * 12345 + 1013904223
    mixed_bits = mixed_bits ^ mixed_bits >> 16
    mixed_bits = mixed_bits * 73244475
    mixed_bits = mixed_bits ^ mixed_bits >> 16
    return (1 - 2 * (mixed_bits >> 7 & 1)).astype(jnp.float32)


def count_sketch(pieces, seed_value, width, sketch_scale):
    flat = jnp.concatenate([piece.reshape(-1) for piece in pieces]).reshape(-1, width)
    signed = flat * sketch_signs(seed_value, flat.shape[0], width)
    return jnp.sum(signed, axis=0) * sketch_scale


def text_grads(text_hidden, text_value, text_states, up_text):
    highest = lax.Precision.HIGHEST
    text_up_grad = jnp.dot(text_hidden.T, text_value, precision=highest)
    text_back = jnp.dot(text_value, up_text.astype(jnp.float32).T, precision=highest)
    text_down_grad = jnp.dot(text_states.astype(jnp.float32).T, text_back, precision=highest)
    return (text_down_grad, text_up_grad)


def per_device(
    clean_latents,
    gaussian_noise,
    text_states,
    queries,
    key_states,
    cotangent,
    text_keys,
    window_radii,
    timestep,
    sketch_seed,
    down_image,
    up_image,
    down_text,
    up_text,
):
    frame_count, row_count, col_count, value_width = queries.shape
    head_count = window_radii.shape[0]
    head_width = value_width // head_count
    col_tiles = col_count // TW
    score_scale = head_width ** (-0.5)
    frame_tile = lax.axis_index("tm")
    row_tile = lax.axis_index("height")
    frame_tiles = lax.axis_size("tm")
    row_tiles = lax.axis_size("height")
    pad_spec = ((0, 0), (0, 0), (TW, TW), (0, 0))
    key_pad = jnp.pad(padded_2(key_states, (("tm", 0), ("height", 1)), frame_count), pad_spec)
    own_q = tile_rows(queries, TW)
    own_c = tile_rows(cotangent, TW)
    head_ids = jnp.arange(head_count, dtype=jnp.int32)

    def head_mask(head_index):
        return window_mask(
            window_radii[head_index],
            frame_tile,
            row_tile,
            frame_tiles,
            row_tiles,
            col_tiles,
            frame_count,
            row_count,
            TW,
        )

    def forward(head_index):
        offset = head_index * head_width
        allowed = head_mask(head_index)
        query_head = lax.dynamic_slice_in_dim(own_q, offset, head_width, 2)
        cot_head = lax.dynamic_slice_in_dim(own_c, offset, head_width, 2)
        key_region = region_rows(lax.dynamic_slice_in_dim(key_pad, offset, head_width, 3), TW)
        text_head = lax.dynamic_slice_in_dim(text_keys, offset, head_width, 1)
        image_scores, log_total, text_part = forward_head(
            query_head, key_region, text_head, cot_head, allowed, score_scale
        )
        image_probs = jnp.exp(image_scores - log_total[..., None]).astype(jnp.bfloat16)
        spread = jnp.einsum(
            "cql,cqd->cld", image_probs, cot_head, preferred_element_type=jnp.float32
        )
        return (text_part, place_back(spread, frame_count, row_count, TW))

    text_part, head_out = lax.map(forward, head_ids)
    text_value = jnp.transpose(text_part, (1, 0, 2)).reshape(-1, value_width)
    middle = head_out[:, :, row_count : 2 * row_count]
    for direction, border in (
        (-1, head_out[:, :, :row_count]),
        (1, head_out[:, :, 2 * row_count :]),
    ):
        middle = middle + shifted(border.astype(jnp.bfloat16), "height", direction).astype(
            border.dtype
        )
    own_part = middle[:, frame_count : 2 * frame_count]
    for direction, border in ((-1, middle[:, :frame_count]), (1, middle[:, 2 * frame_count :])):
        own_part = own_part + shifted(border.astype(jnp.bfloat16), "tm", direction).astype(
            border.dtype
        )
    value_f32 = jnp.transpose(own_part, (1, 2, 3, 0, 4)).reshape(
        frame_count, row_count, col_count, value_width
    )
    value_grad = value_f32.astype(jnp.bfloat16)
    noise_level = timestep[0].astype(jnp.float32) / 1000.0
    mixed = (
        (1.0 - noise_level) * clean_latents.astype(jnp.float32)
        + noise_level * gaussian_noise.astype(jnp.float32)
    ).astype(jnp.bfloat16)
    mixed = mixed.reshape(-1, mixed.shape[3])
    flat_value = value_grad.reshape(-1, value_width)
    hidden = jnp.dot(mixed, down_image, preferred_element_type=jnp.float32).astype(jnp.bfloat16)
    grad_up = lax.dot_general(
        hidden, flat_value, (((0,), (0,)), ((), ())), preferred_element_type=jnp.float32
    )
    backward_low = lax.dot_general(
        flat_value, up_image, (((1,), (1,)), ((), ())), preferred_element_type=jnp.float32
    ).astype(jnp.bfloat16)
    grad_down = lax.dot_general(
        mixed, backward_low, (((0,), (0,)), ((), ())), preferred_element_type=jnp.float32
    )
    text_hidden = jnp.dot(text_states, down_text, preferred_element_type=jnp.float32)
    token_total = frame_count * row_count * col_count * frame_tiles * row_tiles
    param_total = 2 * grad_down.size + 2 * grad_up.size
    sketch_scale = (token_total * (param_total // SKETCH)) ** (-0.5)
    text_down_grad, text_up_grad = text_grads(text_hidden, text_value, text_states, up_text)
    local_sketch = count_sketch(
        (grad_down, grad_up, text_down_grad, text_up_grad), sketch_seed[0], SKETCH, sketch_scale
    )
    grad_sketch = lax.psum(local_sketch, ("tm", "height"))
    return (value_grad, grad_sketch)


def solution(mesh):
    return jax.shard_map(
        per_device,
        mesh=mesh,
        in_specs=(
            P("tm", "height", None, None),
            P("tm", "height", None, None),
            P(),
            P("tm", "height", None, None),
            P("tm", "height", None, None),
            P("tm", "height", None, None),
            P(),
            P(),
            P(),
            P(),
            P(),
            P(),
            P(),
            P(),
        ),
        out_specs=(P("tm", "height", None, None), P()),
        check_vma=False,
    )
```

profile of v0, /device:TPU:1, one launch (start us, length us, event | category | flops | bytes accessed | tf_op | source)
XLA Modules:
  0.0 920.2 jit_solution(15900157499959258757)
XLA Ops:
  7.2 5.1 collective-permute-start
  14.2 7.3 collective-permute-done
  22.5 2.1 constant_dynamic-update-slice_fusion.1
  28.1 12.5 %collective-permute-start.2 = (bf16[12,4,16,1536]{3,2,1,0:T(8,128)(2,1)}, bf16[12,4,16,1536]{3,2,1,0:T(8,128)(2,1)}, u32[]{:S(2)}, u32[]{:S(2)}) collective-permute-start(bf16[12,4,16,1536]{3,2,1,0:T(8,128)(2,1)} %constant_dynamic-update-slice_fusion), channel_id=1, source_target_pairs={{0,1},{1,2},{2,3},{3,4},{4,5},{5,6},{6,7},{7,8},{8,9},{9,10},{10,1... | collective-permute-start | bytes 7077896 | tf_op jit(solution)/shard_map/ppermute | solution.py:15
  40.7 2.1 copy.51
  42.8 97.1 %collective-permute-done.3 = bf16[12,4,16,1536]{3,2,1,0:T(8,128)(2,1)} collective-permute-done((bf16[12,4,16,1536]{3,2,1,0:T(8,128)(2,1)}, bf16[12,4,16,1536]{3,2,1,0:T(8,128)(2,1)}, u32[]{:S(2)}, u32[]{:S(2)}) %collective-permute-start.3) | collective-permute-done | bytes 2359328 | tf_op jit(solution)/shard_map/ppermute | solution.py:18
  139.9 9.7 %fusion.52 = bf16[12,12,32,1536]{3,2,1,0:T(8,128)(2,1)} fusion(bf16[12,4,16,1536]{3,2,1,0:T(8,128)(2,1)} %collective-permute-done.3, bf16[12,4,16,1536]{3,2,1,0:T(8,128)(2,1)} %constant_dynamic-update-slice_fusion, bf16[12,4,16,1536]{3,2,1,0:T(8,128)(2,1)} %collective-permute-done.2), kind=kLoop, calls=%fused_computation.99 | loop fusion | flops 84934656 | bytes 21233664 | tf_op jit(solution)/shard_map/concatenate | solution.py:19
  149.6 213.1 %while.15 = (s32[]{:T(128)}, f32[12,256,128]{1,2,0:T(8,128)}, f32[12,12,12,16,128]{4,3,2,1,0:T(8,128)}, s32[12]{0:T(128)S(1)}, bf16[2,128,1536]{2,1,0:T(8,128)(2...) while((s32[]{:T(128)}, f32[12,256,128]{1,2,0:T(8,128)}, ...), condition=%wide.region_5.6_spmd, body=%wide.region_0.5_spmd.sunk | while | flops 499376128 | bytes 40042176 | solution.py:185
  258.5 2.0 dynamic-slice_bitcast_fusion.4
  362.7 9.7 %convert.8 = bf16[12,12,12,16,128]{4,3,2,1,0:T(8,128)(2,1)} convert(f32[12,12,12,16,128]{4,3,2,1,0:T(8,128)} %get-tuple-element.191) | non-fusion elementwise | flops 3538944 | bytes 21233664 | tf_op jit(solution)/shard_map/convert.3
  372.4 6.3 fusion.75
  378.7 42.7 %collective-permute-start.5 = (bf16[12,12,4,16,128]{4,3,2,1,0:T(8,128)(2,1)}, bf16[12,12,4,16,128]{4,3,2,1,0:T(8,128)(2,1)}, u32[]{:S(2)}, u32[]{:S(2)}) collective-permute-start(bf16[12,12,4,16,128]{4,3,2,1,0:T(8,128)(2,1)} %get-tuple-element.230), channel_id=1, source_target_pairs={{0,1},{1,2},{2,3},{3,4},{4,5},{5,6},{6,7},{7,8},{8,9},{9,10},{10,1... | collective-permute-start | bytes 7077896 | tf_op jit(solution)/shard_map/ppermute | solution.py:26
  424.5 2.6 add_convert_fusion
  427.1 34.4 %collective-permute-done.5 = bf16[12,12,4,16,128]{4,3,2,1,0:T(8,128)(2,1)} collective-permute-done((bf16[12,12,4,16,128]{4,3,2,1,0:T(8,128)(2,1)}, bf16[12,12,4,16,128]{4,3,2,1,0:T(8,128)(2,1)}, u32[]{:S(2)}, u32[]{:S(2)}) %collective-permute-start.5) | collective-permute-done | bytes 2359328 | tf_op jit(solution)/shard_map/ppermute | solution.py:26
  461.5 108.8 %collective-permute-done.4 = bf16[12,12,4,16,128]{4,3,2,1,0:T(8,128)(2,1)} collective-permute-done((bf16[12,12,4,16,128]{4,3,2,1,0:T(8,128)(2,1)}, bf16[12,12,4,16,128]{4,3,2,1,0:T(8,128)(2,1)}, u32[]{:S(2)}, u32[]{:S(2)}) %collective-permute-start.4) | collective-permute-done | bytes 2359328 | tf_op jit(solution)/shard_map/ppermute | solution.py:26
  570.3 7.4 fusion.71
  579.3 61.7 %collective-permute-start.7 = (bf16[12,4,4,16,128]{4,3,2,1,0:T(8,128)(2,1)}, bf16[12,4,4,16,128]{4,3,2,1,0:T(8,128)(2,1)}, u32[]{:S(2)}, u32[]{:S(2)}) collective-permute-start(bf16[12,4,4,16,128]{4,3,2,1,0:T(8,128)(2,1)} %get-tuple-element.232), channel_id=1, source_target_pairs={{0,32},{32,64},{64,96},{96,128},{128,160},{160,192},{192,224},{1,3... | collective-permute-start | bytes 2359304 | tf_op jit(solution)/shard_map/ppermute | solution.py:26
  641.1 2.1 collective-permute-start.6
  644.6 2.0 fusion.77
  650.9 3.8 collective-permute-done.6
  654.7 2.2 fusion.54
  659.3 2.2 fusion.55
  662.2 3.7 fusion.56
  672.2 239.7 %all-reduce.5.cloned.1.call-done = f32[16384]{0:T(1024)} async-done(((f32[16384]{0:T(1024)}), f32[16384]{0:T(1024)}) %all-reduce.5.cloned.1.call-update) | async-done | bytes 65552 | tf_op jit(solution)/shard_map/psum | solution.py:229
  (336 shorter events, 206.4 us)
Async XLA Ops:
  7.2 416.8 %copy-start = (bf16[256,3072]{1,0:T(8,128)(2,1)S(1)}, bf16[256,3072]{1,0:T(8,128)(2,1)}, u32[]{:S(2)}) copy-start(bf16[256,3072]{1,0:T(8,128)(2,1)} %param.18) | copy-start | bytes 4718596
  7.2 33.5 %copy-start.6 = (bf16[4,4,16,1536]{3,2,1,0:T(8,128)(2,1)S(1)}, bf16[4,4,16,1536]{3,2,1,0:T(8,128)(2,1)}, u32[]{:S(2)}) copy-start(bf16[4,4,16,1536]{3,2,1,0:T(8,128)(2,1)} %param.19) | copy-start | bytes 2359300
  7.2 904.7 %all-reduce.5.cloned.1.call-start = ((), (), s32[]{:S(2)}) async-start(), calls=%async_computation | async-start | bytes 131072 | tf_op jit(solution)/shard_map/psum | solution.py:229
  7.2 14.3 %collective-permute-start = (bf16[4,4,16,1536]{3,2,1,0:T(8,128)(2,1)}, bf16[4,4,16,1536]{3,2,1,0:T(8,128)(2,1)S(1)}, u32[]{:S(2)}, u32[]{:S(2)}) collective-permute-start(bf16[4,4,16,1536]{3,2,1,0:T(8,128)(2,1)} %param.20), channel_id=1, source_target_pairs={{0,32},{32,64},{64,96},{96,128},{128,160},{160,192},{192,224},{1,3... | collective-permute-start | bytes 2359304 | tf_op jit(solution)/shard_map/ppermute | solution.py:15
  12.3 13.5 %collective-permute-start.1 = (bf16[4,4,16,1536]{3,2,1,0:T(8,128)(2,1)}, bf16[4,4,16,1536]{3,2,1,0:T(8,128)(2,1)S(1)}, u32[]{:S(2)}, u32[]{:S(2)}) collective-permute-start(bf16[4,4,16,1536]{3,2,1,0:T(8,128)(2,1)} %param.20), channel_id=1, source_target_pairs={{32,0},{64,32},{96,64},{128,96},{160,128},{192,160},{224,192},{33,... | collective-permute-start | bytes 2359304 | tf_op jit(solution)/shard_map/ppermute | solution.py:18
  26.8 113.1 %collective-permute-start.3 = (bf16[12,4,16,1536]{3,2,1,0:T(8,128)(2,1)}, bf16[12,4,16,1536]{3,2,1,0:T(8,128)(2,1)}, u32[]{:S(2)}, u32[]{:S(2)}) collective-permute-start(bf16[12,4,16,1536]{3,2,1,0:T(8,128)(2,1)} %constant_dynamic-update-slice_fusion), channel_id=1, source_target_pairs={{1,0},{2,1},{3,2},{4,3},{5,4},{6,5},{7,6},{8,7},{9,8},{10,9},{11,1... | collective-permute-start | bytes 7077896 | tf_op jit(solution)/shard_map/ppermute | solution.py:18
  28.1 111.8 %collective-permute-start.2 = (bf16[12,4,16,1536]{3,2,1,0:T(8,128)(2,1)}, bf16[12,4,16,1536]{3,2,1,0:T(8,128)(2,1)}, u32[]{:S(2)}, u32[]{:S(2)}) collective-permute-start(bf16[12,4,16,1536]{3,2,1,0:T(8,128)(2,1)} %constant_dynamic-update-slice_fusion), channel_id=1, source_target_pairs={{0,1},{1,2},{2,3},{3,4},{4,5},{5,6},{6,7},{7,8},{8,9},{9,10},{10,1... | collective-permute-start | bytes 7077896 | tf_op jit(solution)/shard_map/ppermute | solution.py:15
  42.8 106.8 %copy-start.9 = (s32[12,3]{0,1:T(4,128)S(1)}, s32[12,3]{0,1:T(4,128)}, u32[]{:S(2)}) copy-start(s32[12,3]{0,1:T(4,128)} %param.23) | copy-start | bytes 436
  167.3 4.4 copy-start.4
  185.1 4.5 copy-start.4
  238.3 4.3 copy-start.4
  256.1 4.5 copy-start.4
  273.9 4.3 copy-start.4
  309.3 4.4 copy-start.4
  327.1 4.4 copy-start.4
  344.9 4.4 copy-start.4
  372.4 51.6 %copy-start.8 = (bf16[3072,16]{0,1:T(8,128)(2,1)S(1)}, bf16[3072,16]{0,1:T(8,128)(2,1)}, u32[]{:S(2)}) copy-start(bf16[3072,16]{0,1:T(8,128)(2,1)} %param.28) | copy-start | bytes 294916
  378.7 82.8 %collective-permute-start.5 = (bf16[12,12,4,16,128]{4,3,2,1,0:T(8,128)(2,1)}, bf16[12,12,4,16,128]{4,3,2,1,0:T(8,128)(2,1)}, u32[]{:S(2)}, u32[]{:S(2)}) collective-permute-start(bf16[12,12,4,16,128]{4,3,2,1,0:T(8,128)(2,1)} %get-tuple-element.230), channel_id=1, source_target_pairs={{0,1},{1,2},{2,3},{3,4},{4,5},{5,6},{6,7},{7,8},{8,9},{9,10},{10,1... | collective-permute-start | bytes 7077896 | tf_op jit(solution)/shard_map/ppermute | solution.py:26
  421.4 148.9 %collective-permute-start.4 = (bf16[12,12,4,16,128]{4,3,2,1,0:T(8,128)(2,1)}, bf16[12,12,4,16,128]{4,3,2,1,0:T(8,128)(2,1)}, u32[]{:S(2)}, u32[]{:S(2)}) collective-permute-start(bf16[12,12,4,16,128]{4,3,2,1,0:T(8,128)(2,1)} %get-tuple-element.229), channel_id=1, source_target_pairs={{1,0},{2,1},{3,2},{4,3},{5,4},{6,5},{7,6},{8,7},{9,8},{10,9},{11,1... | collective-permute-start | bytes 7077896 | tf_op jit(solution)/shard_map/ppermute | solution.py:26
  577.7 65.5 %copy-start.3 = (f32[12,256,128]{1,2,0:T(8,128)S(1)}, f32[12,256,128]{1,2,0:T(8,128)}, u32[]{:S(2)}) copy-start(f32[12,256,128]{1,2,0:T(8,128)} %get-tuple-element.192) | copy-start | bytes 4718596
  577.7 66.9 %copy-start.10 = (bf16[16,1536]{1,0:T(8,128)(2,1)S(1)}, bf16[16,1536]{1,0:T(8,128)(2,1)}, u32[]{:S(2)}) copy-start(bf16[16,1536]{1,0:T(8,128)(2,1)} %param.29) | copy-start | bytes 147460
  579.3 71.6 %collective-permute-start.7 = (bf16[12,4,4,16,128]{4,3,2,1,0:T(8,128)(2,1)}, bf16[12,4,4,16,128]{4,3,2,1,0:T(8,128)(2,1)}, u32[]{:S(2)}, u32[]{:S(2)}) collective-permute-start(bf16[12,4,4,16,128]{4,3,2,1,0:T(8,128)(2,1)} %get-tuple-element.232), channel_id=1, source_target_pairs={{0,32},{32,64},{64,96},{96,128},{128,160},{160,192},{192,224},{1,3... | collective-permute-start | bytes 2359304 | tf_op jit(solution)/shard_map/ppermute | solution.py:26
  641.1 13.6 %collective-permute-start.6 = (bf16[12,4,4,16,128]{4,3,2,1,0:T(8,128)(2,1)}, bf16[12,4,4,16,128]{4,3,2,1,0:T(8,128)(2,1)}, u32[]{:S(2)}, u32[]{:S(2)}) collective-permute-start(bf16[12,4,4,16,128]{4,3,2,1,0:T(8,128)(2,1)} %get-tuple-element.231), channel_id=1, source_target_pairs={{32,0},{64,32},{96,64},{128,96},{160,128},{192,160},{224,192},{33,... | collective-permute-start | bytes 2359304 | tf_op jit(solution)/shard_map/ppermute | solution.py:26
  662.2 5.5 copy-start.7
  (18 other events, 36.4 us)
Sparse Core Ops, SparseCore 0:
  671.3 240.5 all-reduce.4
where the time goes:
time: 925 us; the launch traced here: 920 us
  waiting for transfers between devices  492 us (53%)
  starting transfers between devices  129 us (14%)
  matrix products  89.3 us (10%)
  other arithmetic  82 us (9%)
  local copies, waits for them, and re-layouts  81.4 us (9%)
  loops' own time  31 us (3%)
  between operations  15.5 us (2%)
    psum x1, waiting for transfers between devices, per_device(): grad_sketch = lax.psum(local_sketch, ('tm', 'height'))  240 us
    ppermute x4, waiting for transfers between devices, shifted(): return lax.ppermute(array, axis, pairs)  147 us
    ppermute x4, starting transfers between devices, shifted(): return lax.ppermute(array, axis, pairs)  108 us
    ppermute x2, waiting for transfers between devices, padded_2(): lax.ppermute(lax.slice_in_dim(block, 0, width, axis=dim), axis, backward)  98.3 us
    reshape x50, local copies, waits for them, and re-layouts, tile_rows(): shaped = block.reshape((frame_count, row_count, col_tiles, width) + rest)  38.7 us
    another operation x1, loops' own time, per_device(): text_part, head_out = lax.map(forward, head_ids)  31 us
    and x12, other arithmetic, window_mask(): inside & (row_tile + row_step >= 0) & (row_tile + row_step < row_tiles)  23 us
    dot_general x12, matrix products, forward(): jnp.einsum('cql,cqd->cld', image_probs, cot_head, preferred_element_type=...  22.2 us
  transfers between devices with their start and end apart: 9, of which 7 were waited for; matrix products, arithmetic and copies ran while one was open for 2% of the time, Pallas kernels for 0%

commit v1 on v0

v1 whole, which is shorter than its diff:
```python
import functools

import jax
import jax.numpy as jnp
from jax import lax
from jax.experimental import pallas as pl
from jax.experimental.pallas import tpu as pltpu
from jax.sharding import PartitionSpec as P

MESH = pl.DeviceIdType.MESH
TW = 8
LANES = 128
SKETCH = 16384
NEG = -1e30
LOG2E = 1.4426950408889634
OWN, PART, FAR = 0, 1, 2
AHEAD = 3


def dot(a, b, ca, cb):
    return lax.dot_general(a, b, (((ca,), (cb,)), ((), ())), preferred_element_type=jnp.float32)


def remote(src, dst, ssem, rsem, device):
    return pltpu.make_async_remote_copy(
        src_ref=src, dst_ref=dst, send_sem=ssem, recv_sem=rsem, device_id=device, device_id_type=MESH
    )


def attention_kernel(
    n_a, n_b, heads, frames, rows,
    meta, closed, q_ref, k_ref, c_ref, tk_ref, vg_ref, tv_ref,
    by_head, kr, gp, ga, gf, gy, gz, vgs, tvs, s_ref, p_ref,
    kz_s, kz_r, ky_s, ky_r, kf_s, kf_r, gf_s, gf_r, gy_s, gy_r, gz_s, gz_r,
):
    n_rows = n_a + n_b
    tile = k_ref.shape[0]
    f = lax.axis_index("tm")
    h = lax.axis_index("height")
    even = lax.rem(h, 2) == 0
    partner = (f, h + 1 - 2 * lax.rem(h, 2))
    step = 2 - 4 * lax.rem(h, 2)
    has_to = (h + step >= 0) & (h + step < rows)
    has_from = (h - step >= 0) & (h - step < rows)
    far_to = (f, jnp.where(has_to, h + step, h))
    far_from = (f, jnp.where(has_from, h - step, h))
    has_low = f > 0
    has_high = f < frames - 1
    low = (jnp.maximum(f - 1, 0), h)
    high = (jnp.minimum(f + 1, frames - 1), h)
    sides = ((low, has_low), (high, has_high))

    barrier = pltpu.get_barrier_semaphore()
    peers = [(low, has_low), (high, has_high)]
    if n_rows:
        peers += [(far_to, has_to), (far_from, has_from)]
        pl.semaphore_signal(barrier, inc=1, device_id=partner, device_id_type=MESH)
    for peer, exists in peers:
        @pl.when(exists)
        def _(peer=peer):
            pl.semaphore_signal(barrier, inc=1, device_id=peer, device_id_type=MESH)

    for n, ref in enumerate((k_ref, q_ref, c_ref, tk_ref)):
        for j in range(heads):
            by_head[n, j] = ref[:, j * LANES:(j + 1) * LANES]

    @pl.loop(0, heads)
    def _(s):
        kr[s, 0] = by_head[0, meta[0, s]]

    for side, exists in enumerate((has_low, has_high)):
        @pl.when(jnp.logical_not(exists))
        def _(side=side):
            @pl.loop(0, heads)
            def _(s):
                for row in range(3):
                    kr[s, 3 * (1 + side) + row] = jnp.zeros((tile, LANES), jnp.bfloat16)

    @pl.when(jnp.logical_not(has_from))
    def _():
        @pl.loop(0, heads)
        def _(s):
            for t in (FAR, 3 + FAR, 6 + FAR):
                kr[s, t] = jnp.zeros((tile, LANES), jnp.bfloat16)

    arrivals = 1 if n_rows else 0
    for peer, exists in peers:
        arrivals = arrivals + jnp.where(exists, 1, 0)
    pl.semaphore_wait(barrier, arrivals)

    def k_cross(s):
        return remote(kr.at[s, OWN], kr.at[s, PART], kz_s.at[s], kz_r.at[s], partner)

    def k_far(s):
        return remote(kr.at[s, PART], kr.at[s, FAR], ky_s.at[s], ky_r.at[s], far_to)

    def k_frame(s, side, row):
        return remote(
            kr.at[s, row], kr.at[s, 3 * (2 - side) + row],
            kf_s.at[s, side, row], kf_r.at[s, 1 - side, row], sides[side][0],
        )

    def k_frame_in(s, side, row):
        return remote(
            kr.at[s, row], kr.at[s, 3 * (1 + side) + row],
            kf_s.at[s, side, row], kf_r.at[s, side, row], sides[side][0],
        )

    def g_frame(s, side, row):
        return remote(
            gp.at[s, 3 * (1 + side) + row], gf.at[s, 1 - side, row],
            gf_s.at[s, side, row], gf_r.at[s, 1 - side, row], sides[side][0],
        )

    def g_frame_in(s, side, row):
        return remote(
            gp.at[s, 3 * (1 + side) + row], gf.at[s, side, row],
            gf_s.at[s, side, row], gf_r.at[s, side, row], sides[side][0],
        )

    def g_far(s):
        return remote(gp.at[s, FAR], gy.at[s], gy_s.at[s], gy_r.at[s], far_from)

    def g_cross(s):
        return remote(gp.at[s, PART], gz.at[s], gz_s.at[s], gz_r.at[s], partner)

    def each_side(fn, extra=None):
        for side in range(2):
            cond = sides[side][1] if extra is None else sides[side][1] & extra

            @pl.when(cond)
            def _(side=side):
                fn(side)

    def row_exists(row):
        return has_from if row == FAR else None

    lane = lax.broadcasted_iota(jnp.int32, (2, 8, tile), 2)
    group = lax.broadcasted_iota(jnp.int32, (2, 8, tile), 0)
    cross_col = jnp.where(lax.rem(lane // TW, 2) != group, 1.0, 0.0)
    to_log2 = jnp.float32(LANES**-0.5 * LOG2E)

    def attend(s, tiles):
        head = meta[0, s]
        q = by_head[1, head]
        bias = cross_col * closed[2, s]
        top = None
        for n, t in enumerate([None] + tiles):
            keys = by_head[3, head] if t is None else kr[s, t]
            sc = dot(keys, q, 1, 1)
            if t is not None:
                limit = bias
                if t // 3:
                    limit = limit + closed[0, s] + jnp.where(sides[t // 3 - 1][1], 0.0, NEG)
                if t % 3:
                    limit = limit + closed[1, s]
                if t % 3 == FAR:
                    limit = limit + jnp.where(has_from, 0.0, NEG)
                sc = (sc.reshape(tile // 16, 2, 8, tile) + limit).reshape(tile, tile)
            s_ref[n * tile:(n + 1) * tile, :] = sc
            m = jnp.max(sc.reshape(tile // 8, 8, tile), axis=0)
            top = m if top is None else jnp.maximum(top, m)
        top = jnp.max(top, axis=0, keepdims=True)
        total = jnp.zeros((8, tile), jnp.float32)
        for n in range(len(tiles) + 1):
            e = jnp.exp2((s_ref[n * tile:(n + 1) * tile, :] - top) * to_log2)
            total = total + jnp.sum(e.reshape(tile // 8, 8, tile), axis=0)
            p_ref[n * tile:(n + 1) * tile, :] = e.astype(jnp.bfloat16)
        total = jnp.sum(total, axis=0, keepdims=True)
        inverse = jnp.transpose(jnp.broadcast_to(1.0 / total, (8, tile)))[:, :1]
        cot = (by_head[2, head].astype(jnp.float32) * inverse).astype(jnp.bfloat16)
        for n, t in enumerate([None] + tiles):
            g = dot(p_ref[n * tile:(n + 1) * tile, :], cot, 1, 0)
            if t is None:
                tvs[s] = g
            elif t < 3:
                ga[s, t] = g
            else:
                gp[s, t] = g.astype(jnp.bfloat16)

    def in_range(i, lo, hi, fn):
        if hi > lo:
            @pl.when((i >= lo) & (i < hi))
            def _():
                fn(i)

    def start_frames(s, row):
        each_side(lambda side: k_frame(s, side, row).start(), row_exists(row))

    def pass_partner(s):
        k_cross(s).wait_recv()

        @pl.when(has_to)
        def _():
            k_far(s).start()
        in_range(s, 0, n_a, lambda s: start_frames(s, PART))

    def pass_far(s):
        @pl.when(has_from)
        def _():
            k_far(s).wait_recv()
        in_range(s, 0, n_a, lambda s: start_frames(s, FAR))

    def frames_in(s, row_list):
        for row in row_list:
            each_side(lambda side: k_frame_in(s, side, row).wait_recv(), row_exists(row))

    def frames_out(s, row_list):
        for row in row_list:
            each_side(lambda side: g_frame(s, side, row).start(), row_exists(row))

    def compute_a(s):
        frames_in(s, range(3))
        attend(s, list(range(9)))
        frames_out(s, (FAR, PART, OWN))

    def compute_b(s):
        attend(s, [0, 1, 2])

    def compute_c(s):
        frames_in(s, [OWN])
        attend(s, [0, 3, 6])
        frames_out(s, [OWN])

    def add_frames(s, row):
        def add(side):
            g_frame_in(s, side, row).wait_recv()
            ga[s, row] = ga[s, row] + gf[s, side, row].astype(jnp.float32)
        each_side(add, row_exists(row))

    def reduce_far(s):
        in_range(s, 0, n_a, lambda s: add_frames(s, FAR))

        @pl.when(has_from)
        def _():
            gp[s, FAR] = ga[s, FAR].astype(jnp.bfloat16)
            g_far(s).start()

    def reduce_partner(s):
        in_range(s, 0, n_a, lambda s: add_frames(s, PART))

        @pl.when(has_to)
        def _():
            g_far(s).wait_recv()
            ga[s, PART] = ga[s, PART] + gy[s].astype(jnp.float32)
        gp[s, PART] = ga[s, PART].astype(jnp.bfloat16)
        g_cross(s).start()

    def finish(s):
        in_range(s, 0, n_a, lambda s: add_frames(s, OWN))
        in_range(s, n_rows, heads, lambda s: add_frames(s, OWN))
        if n_rows:
            @pl.when(s < n_rows)
            def _():
                g_cross(s).wait_recv()
                ga[s, OWN] = ga[s, OWN] + gz[s].astype(jnp.float32)
        vgs[s] = ga[s, OWN].astype(jnp.bfloat16)

    for s in range(min(AHEAD, n_rows)):
        k_cross(s).start()

    @pl.loop(0, heads)
    def _(s):
        in_range(s, 0, n_a, lambda s: start_frames(s, OWN))
        in_range(s, n_rows, heads, lambda s: start_frames(s, OWN))

    @pl.loop(0, heads + 6)
    def _(i):
        in_range(i + AHEAD, 0, n_rows, lambda s: k_cross(s).start())
        in_range(i, 0, n_rows, pass_partner)
        in_range(i - 1, 0, n_rows, pass_far)
        in_range(i - 2, 0, n_a, compute_a)
        in_range(i - 2, n_a, n_rows, compute_b)
        in_range(i - 2, n_rows, heads, compute_c)
        in_range(i - 3, 0, n_rows, reduce_far)
        in_range(i - 4, 0, n_rows, reduce_partner)
        in_range(i - 6, 0, heads, finish)

    for j in range(heads):
        slot = meta[1, j]
        vg_ref[:, j * LANES:(j + 1) * LANES] = vgs[slot]
        tv_ref[:, j * LANES:(j + 1) * LANES] = tvs[slot]

    @pl.loop(0, heads)
    def _(s):
        def sent_rows(s):
            k_cross(s).wait_send()
            g_cross(s).wait_send()

            @pl.when(has_to)
            def _():
                k_far(s).wait_send()

            @pl.when(has_from)
            def _():
                g_far(s).wait_send()

        def sent_frames(s, row_list):
            for row in row_list:
                each_side(lambda side: k_frame(s, side, row).wait_send(), row_exists(row))
                each_side(lambda side: g_frame(s, side, row).wait_send(), row_exists(row))
        in_range(s, 0, n_rows, sent_rows)
        in_range(s, 0, n_a, lambda s: sent_frames(s, range(3)))
        in_range(s, n_rows, heads, lambda s: sent_frames(s, [OWN]))


def attention(n_a, n_b, cid, frames, rows, meta, closed, q, k, c, tk):
    tile, width = k.shape
    heads = width // LANES
    vmem = pl.BlockSpec(memory_space=pltpu.VMEM)
    sem = pltpu.SemaphoreType.DMA
    bf, f32 = jnp.bfloat16, jnp.float32
    box = (tile, LANES)
    return pl.pallas_call(
        functools.partial(attention_kernel, n_a, n_b, heads, frames, rows),
        out_shape=(jax.ShapeDtypeStruct((tile, width), bf), jax.ShapeDtypeStruct((tile, width), f32)),
        in_specs=[pl.BlockSpec(memory_space=pltpu.SMEM)] * 2 + [vmem] * 4,
        out_specs=(vmem, vmem),
        scratch_shapes=[
            pltpu.VMEM((4, heads) + box, bf),
            pltpu.VMEM((heads, 9) + box, bf),
            pltpu.VMEM((heads, 9) + box, bf),
            pltpu.VMEM((heads, 3) + box, f32),
            pltpu.VMEM((heads, 2, 3) + box, bf),
            pltpu.VMEM((heads,) + box, bf),
            pltpu.VMEM((heads,) + box, bf),
            pltpu.VMEM((heads,) + box, bf),
            pltpu.VMEM((heads,) + box, f32),
            pltpu.VMEM((10 * tile, tile), f32),
            pltpu.VMEM((10 * tile, tile), bf),
            sem((heads,)), sem((heads,)), sem((heads,)), sem((heads,)),
            sem((heads, 2, 3)), sem((heads, 2, 3)), sem((heads, 2, 3)), sem((heads, 2, 3)),
            sem((heads,)), sem((heads,)), sem((heads,)), sem((heads,)),
        ],
        compiler_params=pltpu.CompilerParams(
            collective_id=cid, has_side_effects=True, vmem_limit_bytes=56 << 20
        ),
    )(meta, closed, q, k, c, tk)


def split2(x):
    hi = x.astype(jnp.bfloat16)
    return hi, (x - hi.astype(jnp.float32)).astype(jnp.bfloat16)


def sketch_kernel(
    token_total,
    time_ref, seed_ref, vg_ref, tv_ref, clean_ref, noise_ref, text_ref,
    di_ref, ui_ref, dt_ref, ut_ref, out_ref,
    flat, part, box1, box2, s_sem, r_sem,
):
    f = lax.axis_index("tm")
    h = lax.axis_index("height")
    g = 2 * f + lax.rem(h, 2)
    w = h // 2
    count = 16

    def in_ring(i):
        return (i // 2, 2 * w + lax.rem(i, 2))

    def in_plane(i):
        return (f, 2 * i + lax.rem(h, 2))

    barrier = pltpu.get_barrier_semaphore()

    @pl.loop(1, count)
    def _(k):
        pl.semaphore_signal(barrier, inc=1, device_id=in_ring(lax.rem(g + k, count)), device_id_type=MESH)
        pl.semaphore_signal(barrier, inc=1, device_id=in_plane(lax.rem(w + k, count)), device_id_type=MESH)

    width = vg_ref.shape[1]
    depth = clean_ref.shape[1]
    rank = ui_ref.shape[0]
    copies = LANES // rank
    level = jnp.full((1, depth), time_ref[0], jnp.int32).astype(jnp.float32) / 1000.0
    mixed = (
        (1.0 - level) * clean_ref[...].astype(jnp.float32) + level * noise_ref[...].astype(jnp.float32)
    ).astype(jnp.bfloat16)
    vg = vg_ref[...]
    hidden = dot(mixed, di_ref[...], 1, 0).astype(jnp.bfloat16)
    up_image = dot(hidden, vg, 0, 0)
    ui_wide = jnp.concatenate([ui_ref[...]] * copies, axis=0)
    ut_wide = jnp.concatenate([ut_ref[...]] * copies, axis=0)
    back = dot(vg, ui_wide, 1, 1).astype(jnp.bfloat16)
    lane8 = lax.broadcasted_iota(jnp.int32, (1, copies, LANES), 2)
    row8 = lax.broadcasted_iota(jnp.int32, (1, copies, LANES), 1)
    pick = lane8 // rank == row8

    def place_down(base, wide):
        kept = jnp.where(pick, wide.reshape(-1, copies, LANES), 0.0)
        flat[base:base + depth // copies, :] = jnp.sum(kept, axis=1)

    def place_up(base, grad):
        per = width // LANES
        for r in range(rank):
            for m in range(per):
                row = base + r * per + m
                flat[row:row + 1, :] = grad[r:r + 1, m * LANES:(m + 1) * LANES]

    place_down(0, dot(mixed, back, 0, 0))
    place_up(384, up_image)
    text = text_ref[...]
    tv_hi, tv_lo = split2(tv_ref[...])
    th_hi, th_lo = split2(dot(text, dt_ref[...], 1, 0))
    place_up(960, dot(th_hi, tv_hi, 0, 0) + (dot(th_hi, tv_lo, 0, 0) + dot(th_lo, tv_hi, 0, 0)))
    tb_hi, tb_lo = split2(dot(tv_hi, ut_wide, 1, 1) + dot(tv_lo, ut_wide, 1, 1))
    place_down(576, dot(text, tb_hi, 0, 0) + dot(text, tb_lo, 0, 0))

    total_rows = flat.shape[0]
    pos = lax.broadcasted_iota(jnp.int32, (total_rows, LANES), 0) * LANES
    pos = pos + lax.broadcasted_iota(jnp.int32, (total_rows, LANES), 1)
    bits = pos * 1103515245 + seed_ref[0] * 12345 + 1013904223
    bits = bits ^ (bits >> 16)
    bits = bits * 73244475
    bits = bits ^ (bits >> 16)
    signs = (1 - 2 * ((bits >> 7) & 1)).astype(jnp.float32)
    rows = SKETCH // LANES
    pieces = total_rows // rows
    scale = (token_total * pieces) ** -0.5
    signed = flat[...] * signs
    acc = signed[0:rows]
    for m in range(1, pieces):
        acc = acc + signed[m * rows:(m + 1) * rows]
    chunk = rows // count
    part[...] = (acc * scale).reshape(count, chunk, LANES)

    pl.semaphore_wait(barrier, 2 * (count - 1))

    def send1(k):
        i = lax.rem(g + k, count)
        return remote(part.at[i], box1.at[g], s_sem.at[0, k], r_sem.at[0, g], in_ring(i))

    def send2(k):
        i = lax.rem(w + k, count)
        return remote(box2.at[w], box2.at[w], s_sem.at[1, k], r_sem.at[1, w], in_plane(i))

    def send3(k):
        i = lax.rem(g + k, count)
        return remote(out_ref.at[g], out_ref.at[g], s_sem.at[2, k], r_sem.at[2, g], in_ring(i))

    def recv(phase, dst, i):
        return remote(dst.at[i], dst.at[i], s_sem.at[phase, 0], r_sem.at[phase, i], in_ring(lax.rem(g + 1, count)))

    def phase(n, me, dst, send):
        @pl.loop(1, count)
        def _(k):
            send(k).start()

        @pl.loop(1, count)
        def _(k):
            recv(n, dst, lax.rem(me + k, count)).wait_recv()

    box1[g] = part[g]
    phase(0, g, box1, send1)
    box2[w] = jnp.sum(box1[...], axis=0)
    phase(1, w, box2, send2)
    out_ref[g] = jnp.sum(box2[...], axis=0)
    phase(2, g, out_ref, send3)

    @pl.loop(1, count)
    def _(k):
        send1(k).wait_send()
        send2(k).wait_send()
        send3(k).wait_send()


def sketch(cid, token_total, *args):
    vmem = pl.BlockSpec(memory_space=pltpu.VMEM)
    smem = pl.BlockSpec(memory_space=pltpu.SMEM)
    rows = SKETCH // LANES
    f32 = jnp.float32
    return pl.pallas_call(
        functools.partial(sketch_kernel, token_total),
        out_shape=jax.ShapeDtypeStruct((16, rows // 16, LANES), f32),
        in_specs=[smem, smem] + [vmem] * 9,
        out_specs=vmem,
        scratch_shapes=[
            pltpu.VMEM((9 * rows, LANES), f32),
            pltpu.VMEM((16, rows // 16, LANES), f32),
            pltpu.VMEM((16, rows // 16, LANES), f32),
            pltpu.VMEM((16, rows // 16, LANES), f32),
            pltpu.SemaphoreType.DMA((3, 16)),
            pltpu.SemaphoreType.DMA((3, 16)),
        ],
        compiler_params=pltpu.CompilerParams(
            collective_id=cid, has_side_effects=True, vmem_limit_bytes=56 << 20
        ),
    )(*args)


VARIANTS = ((12, 0),)


def assign(radii, variants, heads):
    far_f = radii[:, 0] > 0
    far_r = radii[:, 1] > 0
    kind = jnp.where(far_r, jnp.where(far_f, 0, 1), jnp.where(far_f, 2, 3))
    n = [jnp.sum(kind == t) for t in range(4)]
    choice = jnp.int32(len(variants) - 1)
    a, b = jnp.int32(variants[-1][0]), jnp.int32(variants[-1][1])
    for i in reversed(range(len(variants) - 1)):
        va, vb = variants[i]
        vc = heads - va - vb
        fits = (n[0] <= va) & (n[0] + n[1] <= va + vb) & (n[0] + n[2] <= va + vc)
        choice = jnp.where(fits, i, choice)
        a, b = jnp.where(fits, va, a), jnp.where(fits, vb, b)
    c = heads - a - b
    before = jnp.tril(jnp.ones((heads, heads), jnp.int32), -1)
    rank = jnp.sum(before * (kind[:, None] == kind[None, :]), axis=1)
    over_b = jnp.maximum(n[1] - b, 0)
    over_c = jnp.maximum(n[2] - c, 0)
    spare_a = a - n[0] - over_b - over_c
    spare_b = b - (n[1] - over_b)
    slot_a = rank
    slot_b = jnp.where(rank < over_b, n[0] + rank, a + rank - over_b)
    slot_c = jnp.where(rank < over_c, n[0] + over_b + rank, heads - (n[2] - over_c) + rank - over_c)
    slot_d = jnp.where(
        rank < spare_a,
        n[0] + over_b + over_c + rank,
        jnp.where(rank < spare_a + spare_b, a + (n[1] - over_b) + rank - spare_a, a + b + rank - spare_a - spare_b),
    )
    slot = jnp.where(kind == 0, slot_a, jnp.where(kind == 1, slot_b, jnp.where(kind == 2, slot_c, slot_d)))
    hit = (slot[None, :] == jnp.arange(heads)[:, None]).astype(jnp.int32)
    table = jnp.concatenate([jnp.arange(heads, dtype=jnp.int32)[:, None], radii.astype(jnp.int32)], axis=1)
    by_slot = jnp.sum(hit[:, :, None] * table[None], axis=1)
    meta = jnp.concatenate([by_slot[:, :1].T, slot[None].astype(jnp.int32)], axis=0)
    closed = jnp.where(by_slot[:, 1:].T > 0, 0.0, NEG)
    return choice, meta, closed


def per_device(
    clean_latents, gaussian_noise, text_states, queries, key_states, cotangent, text_keys,
    window_radii, timestep, sketch_seed, down_image, up_image, down_text, up_text,
):
    width = queries.shape[-1]
    depth = clean_latents.shape[-1]
    heads = window_radii.shape[0]
    frames, rows = lax.axis_size("tm"), lax.axis_size("height")
    choice, meta, closed = assign(window_radii, VARIANTS, heads)
    branches = [
        functools.partial(attention, a, b, i + 1, frames, rows) for i, (a, b) in enumerate(VARIANTS)
    ]
    operands = (
        meta,
        closed,
        queries.reshape(-1, width),
        key_states.reshape(-1, width),
        cotangent.reshape(-1, width),
        text_keys,
    )
    if len(branches) == 1:
        vg, tv = branches[0](*operands)
    else:
        vg, tv = lax.switch(choice, branches, *operands)
    tokens = vg.shape[0] * frames * rows
    sk = sketch(
        0, tokens, timestep, sketch_seed, vg, tv,
        clean_latents.reshape(-1, depth), gaussian_noise.reshape(-1, depth), text_states,
        down_image, up_image, down_text, up_text,
    )
    return vg.reshape(queries.shape), sk.reshape(-1)


def solution(mesh):
    block = P("tm", "height", None, None)
    return jax.shard_map(
        per_device,
        mesh=mesh,
        in_specs=(block, block, P(), block, block, block) + (P(),) * 8,
        out_specs=(block, P()),
        check_vma=False,
    )
```

time: 925 us -> 184 us (0.20)
  waiting for transfers between devices: 492 us -> 0 us
  Pallas kernels: 0 us -> 167 us
  starting transfers between devices: 129 us -> 0 us
  matrix products: 89.3 us -> 0 us
  other arithmetic: 82 us -> 5.16 us
  local copies, waits for them, and re-layouts: 81.4 us -> 5.92 us
  loops' own time: 31 us -> 0 us
  between operations: 15.5 us -> 6 us
    ppermute x8 -> x0, waiting for transfers between devices: 253 us -> none  [the longest x4 147 us: shifted(): return lax.ppermute(array, axis, pairs)]
    psum x1 -> x0, waiting for transfers between devices: 240 us -> none  [per_device(): grad_sketch = lax.psum(local_sketch, ('tm', 'height'))]
    pallas_call x0 -> x2, Pallas kernels: none -> 167 us  [the longest x1 133 us: attention(): pl.pallas_call(functools.partial(attention_kernel, n_a, n_b, heads, frame...]
    ppermute x8 -> x0, starting transfers between devices: 129 us -> none  [the longest x4 108 us: shifted(): return lax.ppermute(array, axis, pairs)]
    dot_general x54 -> x0, matrix products: 89.3 us -> none  [the longest x12 22.2 us: forward(): jnp.einsum('cql,cqd->cld', image_probs, cot_head, preferred_element_type=...]
    reshape x55 -> x0, local copies, waits for them, and re-layouts: 44.2 us -> none  [the longest x50 38.7 us: tile_rows(): shaped = block.reshape((frame_count, row_count, col_tiles, width) + rest)]
    another operation x1 -> x0, loops' own time: 31 us -> none  [per_device(): text_part, head_out = lax.map(forward, head_ids)]
    and x24 -> x0, other arithmetic: 23.6 us -> none  [the longest x12 23 us: window_mask(): inside & (row_tile + row_step >= 0) & (row_tile + row_step < row_tiles)]
  transfers between devices with their start and end apart: 9 -> 0, of which waited for: 7 -> 0; matrix products, arithmetic and copies ran while one was open for 2% -> 0% of each run, Pallas kernels for 0% -> 0%
where the time goes in v1:
time: 184 us
  Pallas kernels  167 us (91%)
  between operations  6 us (3%)
  local copies, waits for them, and re-layouts  5.92 us (3%)
  other arithmetic  5.16 us (3%)
    pallas_call x1, Pallas kernels, attention(): pl.pallas_call(functools.partial(attention_kernel, n_a, n_b, heads, frame...  133 us
    pallas_call x1, Pallas kernels, sketch(): pl.pallas_call(functools.partial(sketch_kernel, token_total), out_shape=j...  33.5 us
    unnamed x9, local copies, waits for them, and re-layouts  5.73 us

profile of v1, /device:TPU:1, one launch (start us, length us, event | category | flops | bytes accessed | tf_op | source)
XLA Modules:
  0.0 184.0 jit_solution(17953731446609826106)
XLA Ops:
  1.9 0.7 pad_add_fusion
  2.6 1.5 fusion.3
  8.1 0.2 select_reduce_fusion
  8.3 0.7 compare_select_fusion.11
  9.0 0.7 bitcast_select_fusion.2
  9.7 0.3 multiply_reduce_fusion
  9.9 0.1 slice_reduce_fusion
  10.1 0.1 slice.17
  10.1 0.1 copy.25
  10.2 0.6 select_bitcast_fusion.closed
  10.8 0.6 pad_add_fusion.1.meta
  11.4 2.0 %copy.23.di_ref = bf16[3072,16]{1,0:T(8,128)(2,1)} copy(bf16[3072,16]{0,1:T(8,128)(2,1)} %param.24) | data formatting | bytes 196608 | tf_op args[10]
  13.4 2.1 %copy.24.dt_ref = bf16[3072,16]{1,0:T(8,128)(2,1)} copy(bf16[3072,16]{0,1:T(8,128)(2,1)} %param.26) | data formatting | bytes 196608 | tf_op args[12]
  15.5 133.4 %shard_map.149 = (bf16[256,1536]{1,0:T(8,128)(2,1)}, f32[256,1536]{1,0:T(8,128)}) custom-call(s32[2,12]{1,0:T(2,128)} %pad_add_fusion.1.meta, f32[3,12]{1,0:T(4,128)} %select_bitcast_fusion.closed, bf16[256,1536]{1,0:T(8,128)(2,1)} %bitcast.52, bf16[256,1536]{1,0:T(8,128)(2,1)} %bitcast.53, bf16[256,1536]{1,0:T(8,128)(2,1)} %bitcast.54, bf16[256,1536]{1,0:T(8,128)(2,1)} %tk_ref.1), custom_call_target="tpu_custom_call" | custom-call | tf_op jit(solution)/shard_map/pallas_call | solution.py:314
  148.9 0.0 copy-start
  148.9 33.5 %shard_map.150 = f32[16,8,128]{2,1,0:T(8,128)} custom-call(s32[1]{0:T(128)S(6)} %copy.28.time_ref, s32[1]{0:T(128)S(6)} %copy.29.seed_ref, bf16[256,1536]{1,0:T(8,128)(2,1)} %get-tuple-element.4.vg_ref, f32[256,1536]{1,0:T(8,128)} %get-tuple-element.5.tv_ref, bf16[256,3072]{1,0:T(8,128)(2,1)} %bitcast.50, bf16[256,3072]{1,0:T(8,128)(2,1)} %bitcast.51, ...), custom_call_target="tpu_custom_call" | custom-call | tf_op jit(solution)/shard_map/pallas_call | solution.py:472
  182.5 0.0 copy-start.1
  182.5 0.0 copy-done
  182.5 0.9 copy.30
  183.4 0.0 copy-done.1
  183.4 0.6 copy.31
  (3 shorter events, 0.0 us)
Async XLA Ops:
  148.9 33.5 %copy-start = (bf16[256,1536]{1,0:T(8,128)(2,1)S(1)}, bf16[256,1536]{1,0:T(8,128)(2,1)}, u32[]{:S(2)}) copy-start(bf16[256,1536]{1,0:T(8,128)(2,1)} %get-tuple-element.4.vg_ref) | copy-start | bytes 2359300
  182.5 0.9 copy-start.1

commit v2 on v1

--- a/solution.py
+++ b/solution.py
@@ -377,7 +377,7 @@
         (1.0 - level) * clean_ref[...].astype(jnp.float32) + level * noise_ref[...].astype(jnp.float32)
     ).astype(jnp.bfloat16)
     vg = vg_ref[...]
-    hidden = dot(mixed, di_ref[...], 1, 0).astype(jnp.bfloat16)
+    hidden = dot(mixed, di_ref[...], 1, 1).astype(jnp.bfloat16)
     up_image = dot(hidden, vg, 0, 0)
     ui_wide = jnp.concatenate([ui_ref[...]] * copies, axis=0)
     ut_wide = jnp.concatenate([ut_ref[...]] * copies, axis=0)
@@ -401,7 +401,7 @@
     place_up(384, up_image)
     text = text_ref[...]
     tv_hi, tv_lo = split2(tv_ref[...])
-    th_hi, th_lo = split2(dot(text, dt_ref[...], 1, 0))
+    th_hi, th_lo = split2(dot(text, dt_ref[...], 1, 1))
     place_up(960, dot(th_hi, tv_hi, 0, 0) + (dot(th_hi, tv_lo, 0, 0) + dot(th_lo, tv_hi, 0, 0)))
     tb_hi, tb_lo = split2(dot(tv_hi, ut_wide, 1, 1) + dot(tv_lo, ut_wide, 1, 1))
     place_down(576, dot(text, tb_hi, 0, 0) + dot(text, tb_lo, 0, 0))
@@ -488,44 +488,66 @@
     )(*args)
 
 
-VARIANTS = ((12, 0),)
-
-
-def assign(radii, variants, heads):
-    far_f = radii[:, 0] > 0
-    far_r = radii[:, 1] > 0
-    kind = jnp.where(far_r, jnp.where(far_f, 0, 1), jnp.where(far_f, 2, 3))
-    n = [jnp.sum(kind == t) for t in range(4)]
-    choice = jnp.int32(len(variants) - 1)
+VARIANTS = ((2, 3), (3, 3), (4, 3), (5, 3), (7, 2), (12, 0))
+
+
+def plan_kernel(variants, heads, radii, choice, meta, closed):
+    kinds = []
+    counts = [jnp.int32(0)] * 4
+    ranks = []
+    for j in range(heads):
+        far_f, far_r = radii[j, 0] > 0, radii[j, 1] > 0
+        kind = jnp.where(far_r, jnp.where(far_f, 0, 1), jnp.where(far_f, 2, 3))
+        kinds.append(kind)
+        rank = jnp.int32(0)
+        for t in range(4):
+            rank = jnp.where(kind == t, counts[t], rank)
+            counts[t] = counts[t] + jnp.where(kind == t, 1, 0)
+        ranks.append(rank)
+    pick = jnp.int32(len(variants) - 1)
     a, b = jnp.int32(variants[-1][0]), jnp.int32(variants[-1][1])
     for i in reversed(range(len(variants) - 1)):
         va, vb = variants[i]
         vc = heads - va - vb
-        fits = (n[0] <= va) & (n[0] + n[1] <= va + vb) & (n[0] + n[2] <= va + vc)
-        choice = jnp.where(fits, i, choice)
+        fits = (counts[0] <= va) & (counts[0] + counts[1] <= va + vb) & (counts[0] + counts[2] <= va + vc)
+        pick = jnp.where(fits, i, pick)
         a, b = jnp.where(fits, va, a), jnp.where(fits, vb, b)
     c = heads - a - b
-    before = jnp.tril(jnp.ones((heads, heads), jnp.int32), -1)
-    rank = jnp.sum(before * (kind[:, None] == kind[None, :]), axis=1)
-    over_b = jnp.maximum(n[1] - b, 0)
-    over_c = jnp.maximum(n[2] - c, 0)
-    spare_a = a - n[0] - over_b - over_c
-    spare_b = b - (n[1] - over_b)
-    slot_a = rank
-    slot_b = jnp.where(rank < over_b, n[0] + rank, a + rank - over_b)
-    slot_c = jnp.where(rank < over_c, n[0] + over_b + rank, heads - (n[2] - over_c) + rank - over_c)
-    slot_d = jnp.where(
-        rank < spare_a,
-        n[0] + over_b + over_c + rank,
-        jnp.where(rank < spare_a + spare_b, a + (n[1] - over_b) + rank - spare_a, a + b + rank - spare_a - spare_b),
-    )
-    slot = jnp.where(kind == 0, slot_a, jnp.where(kind == 1, slot_b, jnp.where(kind == 2, slot_c, slot_d)))
-    hit = (slot[None, :] == jnp.arange(heads)[:, None]).astype(jnp.int32)
-    table = jnp.concatenate([jnp.arange(heads, dtype=jnp.int32)[:, None], radii.astype(jnp.int32)], axis=1)
-    by_slot = jnp.sum(hit[:, :, None] * table[None], axis=1)
-    meta = jnp.concatenate([by_slot[:, :1].T, slot[None].astype(jnp.int32)], axis=0)
-    closed = jnp.where(by_slot[:, 1:].T > 0, 0.0, NEG)
-    return choice, meta, closed
+    over_b = jnp.maximum(counts[1] - b, 0)
+    over_c = jnp.maximum(counts[2] - c, 0)
+    spare_a = a - counts[0] - over_b - over_c
+    spare_b = b - (counts[1] - over_b)
+    choice[0] = pick
+    for j in range(heads):
+        kind, rank = kinds[j], ranks[j]
+        slot_b = jnp.where(rank < over_b, counts[0] + rank, a + rank - over_b)
+        slot_c = jnp.where(rank < over_c, counts[0] + over_b + rank, heads - counts[2] + rank)
+        left = rank - spare_a - spare_b
+        slot_d = jnp.where(
+            rank < spare_a,
+            counts[0] + over_b + over_c + rank,
+            a + b + left,
+        )
+        slot = jnp.where(kind == 0, rank, jnp.where(kind == 1, slot_b, jnp.where(kind == 2, slot_c, slot_d)))
+        meta[0, slot] = j
+        meta[1, j] = slot
+        for r in range(3):
+            closed[r, slot] = jnp.where(radii[j, r] > 0, 0.0, NEG)
+
+
+def plan(radii):
+    heads = radii.shape[0]
+    smem = pl.BlockSpec(memory_space=pltpu.SMEM)
+    return pl.pallas_call(
+        functools.partial(plan_kernel, VARIANTS, heads),
+        out_shape=(
+            jax.ShapeDtypeStruct((1,), jnp.int32),
+            jax.ShapeDtypeStruct((2, heads), jnp.int32),
+            jax.ShapeDtypeStruct((3, heads), jnp.float32),
+        ),
+        in_specs=[smem],
+        out_specs=(smem, smem, smem),
+    )(radii)
 
 
 def per_device(
@@ -534,9 +556,8 @@
 ):
     width = queries.shape[-1]
     depth = clean_latents.shape[-1]
-    heads = window_radii.shape[0]
     frames, rows = lax.axis_size("tm"), lax.axis_size("height")
-    choice, meta, closed = assign(window_radii, VARIANTS, heads)
+    choice, meta, closed = plan(window_radii)
     branches = [
         functools.partial(attention, a, b, i + 1, frames, rows) for i, (a, b) in enumerate(VARIANTS)
     ]
@@ -551,12 +572,12 @@
     if len(branches) == 1:
         vg, tv = branches[0](*operands)
     else:
-        vg, tv = lax.switch(choice, branches, *operands)
+        vg, tv = lax.switch(choice[0], branches, *operands)
     tokens = vg.shape[0] * frames * rows
     sk = sketch(
         0, tokens, timestep, sketch_seed, vg, tv,
         clean_latents.reshape(-1, depth), gaussian_noise.reshape(-1, depth), text_states,
-        down_image, up_image, down_text, up_text,
+        down_image.T, up_image, down_text.T, up_text,
     )
     return vg.reshape(queries.shape), sk.reshape(-1)
 

time: 184 us -> 124 us (0.67)
  Pallas kernels: 167 us -> 117 us
  other arithmetic: 5.16 us -> 0 us
  between operations: 6 us -> 2.6 us
  local copies, waits for them, and re-layouts: 5.92 us -> 3.97 us
    pallas_call x1, Pallas kernels: 133 us -> 86.1 us  [attention(): pl.pallas_call(functools.partial(attention_kernel, n_a, n_b, heads, frame...]
    pallas_call x1, Pallas kernels: 33.5 us -> 29.3 us  [sketch(): pl.pallas_call(functools.partial(sketch_kernel, token_total), out_shape=j...]
    unnamed x9 -> x4, local copies, waits for them, and re-layouts: 5.73 us -> 2.84 us
    reduce_sum x3 -> x0, other arithmetic: 1.97 us -> none  [the longest x1 1.51 us: assign(): n = [jnp.sum(kind == t) for t in range(4)]]
    select_n x3 -> x0, other arithmetic: 1.91 us -> none  [the longest x2 1.31 us: assign(): jnp.where(kind == 0, slot_a, jnp.where(kind == 1, slot_b, jnp.where(kind...]
where the time goes in v2:
time: 124 us
  Pallas kernels  117 us (94%)
  local copies, waits for them, and re-layouts  3.97 us (3%)
  between operations  2.6 us (2%)
    pallas_call x1, Pallas kernels, attention(): pl.pallas_call(functools.partial(attention_kernel, n_a, n_b, heads, frame...  86.1 us
    pallas_call x1, Pallas kernels, sketch(): pl.pallas_call(functools.partial(sketch_kernel, token_total), out_shape=j...  29.3 us
    unnamed x4, local copies, waits for them, and re-layouts  2.84 us

profile of v2, /device:TPU:1, one launch (start us, length us, event | category | flops | bytes accessed | tf_op | source)
XLA Modules:
  0.0 123.7 jit_solution(16219787748228200800)
XLA Ops:
  0.6 1.4 %copy.16.radii = s32[12,3]{1,0:T(8,128)} copy(s32[12,3]{0,1:T(4,128)} %param.27) | data formatting | bytes 288 | tf_op args[7]
  2.0 1.7 %shard_map.149 = (s32[1]{0:T(128)}, s32[2,12]{1,0:T(2,128)S(1)}, f32[3,12]{1,0:T(4,128)S(1)}) custom-call(s32[12,3]{1,0:T(8,128)} %copy.16.radii), custom_call_target="tpu_custom_call" | custom-call | tf_op jit(solution)/shard_map/pallas_call | solution.py:541
  4.4 87.3 %conditional.1 = (bf16[256,1536]{1,0:T(8,128)(2,1)}, f32[256,1536]{1,0:T(8,128)S(1)}, bf16[4,4,16,1536]{3,2,1,0:T(8,128)(2,1)S(1)}) conditional(s32[]{:T(128)} %bitcast, (s32[2,12]{1,0:T(2,128)S(1)}, f32[3,12]{1,0:T(4,128)S(1)}, bf16[256,1536]{1,0:T(8,128)(2,1)}, bf16[256,1536]{1,0:T(8,128)(2,1)}, ...), branch_computations={%region_0.0_spmd.clone, %region_1.0_spmd.clone, %region_2.0_spmd.c... | conditional | bytes 1572888 | solution.py:575
  4.4 86.1 %branch_2_fun.2 = (bf16[256,1536]{1,0:T(8,128)(2,1)}, f32[256,1536]{1,0:T(8,128)S(1)}) custom-call(s32[2,12]{1,0:T(2,128)S(1)} %get-tuple-element.187.meta, f32[3,12]{1,0:T(4,128)S(1)} %get-tuple-element.188.closed, bf16[256,1536]{1,0:T(8,128)(2,1)} %get-tuple-element.189.q_ref, bf16[256,1536]{1,0:T(8,128)(2,1)} %get-tuple-element.190.k_ref, ...), custom_call_target="tpu_custom_call" | custom-call | tf_op jit(solution)/shard_map/cond/branch_2_fun/pallas_call | solution.py:314
  90.5 1.1 copy.25
  91.6 0.0 copy-start
  92.9 29.3 %shard_map.150 = f32[16,8,128]{2,1,0:T(8,128)} custom-call(s32[1]{0:T(128)S(6)} %copy.36.time_ref, s32[1]{0:T(128)S(6)} %copy.37.seed_ref, bf16[256,1536]{1,0:T(8,128)(2,1)} %get-tuple-element.165.vg_ref, f32[256,1536]{1,0:T(8,128)S(1)} %get-tuple-element.166.tv_ref, bf16[256,3072]{1,0:T(8,128)(2,1)} %bitcast.33, bf16[256,3072]{1,0:T(8,128)(2,1)} %bitcast.34, ...), custom_call_target="tpu_custom_call" | custom-call | tf_op jit(solution)/shard_map/pallas_call | solution.py:472
  122.3 0.0 copy-done
  122.3 1.5 %copy.38 = f32[16384]{0:T(1024)} copy(f32[16384]{0:T(1024)} %bitcast.35) | data formatting | bytes 131072
Async XLA Ops:
  91.6 30.6 %copy-start = (bf16[4,4,16,1536]{3,2,1,0:T(8,128)(2,1)}, bf16[4,4,16,1536]{3,2,1,0:T(8,128)(2,1)S(1)}, u32[]{:S(2)}) copy-start(bf16[4,4,16,1536]{3,2,1,0:T(8,128)(2,1)S(1)} %get-tuple-element.260) | copy-start | bytes 2359300

commit v3 on v2

v3 whole, which is shorter than its diff:
```python
import functools

import jax
import jax.numpy as jnp
from jax import lax
from jax.experimental import pallas as pl
from jax.experimental.pallas import tpu as pltpu
from jax.sharding import PartitionSpec as P

MESH = pl.DeviceIdType.MESH
TW = 8
LANES = 128
SKETCH = 16384
NEG = -1e30
LOG2E = 1.4426950408889634
OWN, PART, FAR = 0, 1, 2
AHEAD = 3


def dot(a, b, ca, cb):
    return lax.dot_general(a, b, (((ca,), (cb,)), ((), ())), preferred_element_type=jnp.float32)


def remote(src, dst, ssem, rsem, device):
    return pltpu.make_async_remote_copy(
        src_ref=src, dst_ref=dst, send_sem=ssem, recv_sem=rsem, device_id=device, device_id_type=MESH
    )


def attention_kernel(
    n_a, n_b, heads, frames, rows, token_total,
    meta, closed, time_ref, seed_ref, k_ref, ui_ref, ut_ref, di_ref, dt_ref,
    q_hbm, c_hbm, tk_hbm, clean_hbm, noise_hbm, text_hbm, vg_ref, out_ref,
    q_ref, c_ref, tk_ref, clean_ref, noise_ref, text_ref, l_sem,
    mixed_t, hid_t, text_hid, ui_wide, back, up_s, flat, signs, part, box1, box2, a_s, a_r,
    by_head, kr, gp, ga, gf, gy, gz, vgs, tvs, s_ref, p_ref,
    kz_s, kz_r, ky_s, ky_r, kf_s, kf_r, gf_s, gf_r, gy_s, gy_r, gz_s, gz_r,
):
    n_rows = n_a + n_b
    tile = k_ref.shape[0]
    f = lax.axis_index("tm")
    h = lax.axis_index("height")
    even = lax.rem(h, 2) == 0
    partner = (f, h + 1 - 2 * lax.rem(h, 2))
    step = 2 - 4 * lax.rem(h, 2)
    has_to = (h + step >= 0) & (h + step < rows)
    has_from = (h - step >= 0) & (h - step < rows)
    far_to = (f, jnp.where(has_to, h + step, h))
    far_from = (f, jnp.where(has_from, h - step, h))
    has_low = f > 0
    has_high = f < frames - 1
    low = (jnp.maximum(f - 1, 0), h)
    high = (jnp.minimum(f + 1, frames - 1), h)
    sides = ((low, has_low), (high, has_high))

    g = 2 * f + lax.rem(h, 2)
    w = h // 2
    count = 16

    def in_ring(i):
        return (i // 2, 2 * w + lax.rem(i, 2))

    def in_plane(i):
        return (f, 2 * i + lax.rem(h, 2))

    barrier = pltpu.get_barrier_semaphore()

    @pl.loop(1, count)
    def _(k):
        pl.semaphore_signal(barrier, inc=1, device_id=in_ring(lax.rem(g + k, count)), device_id_type=MESH)
        pl.semaphore_signal(barrier, inc=1, device_id=in_plane(lax.rem(w + k, count)), device_id_type=MESH)

    loads = [
        pltpu.make_async_copy(src, dst, l_sem.at[n])
        for n, (src, dst) in enumerate((
            (q_hbm, q_ref), (c_hbm, c_ref), (tk_hbm, tk_ref),
            (clean_hbm, clean_ref), (noise_hbm, noise_ref), (text_hbm, text_ref),
        ))
    ]
    for load in loads:
        load.start()

    def columns(j, size=LANES):
        return pl.ds(pl.multiple_of(j * size, size), size)

    @pl.loop(0, heads)
    def _(j):
        by_head[0, j] = k_ref[:, columns(j)]

    @pl.loop(0, heads)
    def _(s):
        kr[s, 0] = by_head[0, meta[0, s]]

    for side, exists in enumerate((has_low, has_high)):
        @pl.when(jnp.logical_not(exists))
        def _(side=side):
            @pl.loop(0, heads)
            def _(s):
                for row in range(3):
                    kr[s, 3 * (1 + side) + row] = jnp.zeros((tile, LANES), jnp.bfloat16)

    @pl.when(jnp.logical_not(has_from))
    def _():
        @pl.loop(0, heads)
        def _(s):
            for t in (FAR, 3 + FAR, 6 + FAR):
                kr[s, t] = jnp.zeros((tile, LANES), jnp.bfloat16)

    pl.semaphore_wait(barrier, 2 * (count - 1))

    def k_cross(s):
        return remote(kr.at[s, OWN], kr.at[s, PART], kz_s.at[s], kz_r.at[s], partner)

    def k_far(s):
        return remote(kr.at[s, PART], kr.at[s, FAR], ky_s.at[s], ky_r.at[s], far_to)

    def k_frame(s, side, row):
        return remote(
            kr.at[s, row], kr.at[s, 3 * (2 - side) + row],
            kf_s.at[s, side, row], kf_r.at[s, 1 - side, row], sides[side][0],
        )

    def k_frame_in(s, side, row):
        return remote(
            kr.at[s, row], kr.at[s, 3 * (1 + side) + row],
            kf_s.at[s, side, row], kf_r.at[s, side, row], sides[side][0],
        )

    def g_frame(s, side, row):
        return remote(
            gp.at[s, 3 * (1 + side) + row], gf.at[s, 1 - side, row],
            gf_s.at[s, side, row], gf_r.at[s, 1 - side, row], sides[side][0],
        )

    def g_frame_in(s, side, row):
        return remote(
            gp.at[s, 3 * (1 + side) + row], gf.at[s, side, row],
            gf_s.at[s, side, row], gf_r.at[s, side, row], sides[side][0],
        )

    def g_far(s):
        return remote(gp.at[s, FAR], gy.at[s], gy_s.at[s], gy_r.at[s], far_from)

    def g_cross(s):
        return remote(gp.at[s, PART], gz.at[s], gz_s.at[s], gz_r.at[s], partner)

    def each_side(fn, extra=None):
        for side in range(2):
            cond = sides[side][1] if extra is None else sides[side][1] & extra

            @pl.when(cond)
            def _(side=side):
                fn(side)

    def row_exists(row):
        return has_from if row == FAR else None

    lane = lax.broadcasted_iota(jnp.int32, (2, 8, tile), 2)
    group = lax.broadcasted_iota(jnp.int32, (2, 8, tile), 0)
    cross_col = jnp.where(lax.rem(lane // TW, 2) != group, 1.0, 0.0)
    to_log2 = jnp.float32(LANES**-0.5 * LOG2E)

    def attend(s, tiles):
        head = meta[0, s]
        q = by_head[1, head]
        bias = cross_col * closed[2, s]
        low_limit = closed[0, s] + jnp.where(has_low, 0.0, NEG)
        high_limit = closed[0, s] + jnp.where(has_high, 0.0, NEG)
        far_limit = closed[1, s] + jnp.where(has_from, 0.0, NEG)
        stride, number = tiles

        def score(n, keys, limit, top):
            sc = dot(keys, q, 1, 1)
            if limit is not None:
                sc = (sc.reshape(tile // 16, 2, 8, tile) + limit).reshape(tile, tile)
            s_ref[n] = sc
            return jnp.maximum(top, jnp.max(sc.reshape(tile // 8, 8, tile), axis=0))

        def score_tile(n, top):
            t = n * stride
            limit = bias
            if t // 3:
                limit = limit + (low_limit, high_limit)[t // 3 - 1]
            if t % 3:
                limit = limit + (closed[1, s], far_limit)[t % 3 - 1]
            return score(n, kr[s, t], limit, top)

        top = score(number, by_head[3, head], None, jnp.full((8, tile), NEG, jnp.float32))
        for n in range(number):
            top = score_tile(n, top)
        top = jnp.max(top, axis=0, keepdims=True)

        def weigh(n, total):
            e = jnp.exp2((s_ref[n] - top) * to_log2)
            p_ref[n] = e.astype(jnp.bfloat16)
            return total + jnp.sum(e.reshape(tile // 8, 8, tile), axis=0)

        total = jnp.zeros((8, tile), jnp.float32)
        for n in range(number + 1):
            total = weigh(n, total)
        total = jnp.sum(total, axis=0, keepdims=True)
        inverse = jnp.transpose(jnp.broadcast_to(1.0 / total, (8, tile)))[:, :1]
        cot = (by_head[2, head].astype(jnp.float32) * inverse).astype(jnp.bfloat16)
        tvs[s] = dot(p_ref[number], cot, 1, 0)

        for n in range(number):
            t = n * stride
            grad = dot(p_ref[n], cot, 1, 0)
            if t < 3:
                ga[s, t] = grad
            else:
                gp[s, t] = grad.astype(jnp.bfloat16)

    def in_range(i, lo, hi, fn):
        if hi > lo:
            @pl.when((i >= lo) & (i < hi))
            def _():
                fn(i)

    def start_frames(s, row):
        each_side(lambda side: k_frame(s, side, row).start(), row_exists(row))

    def pass_partner(s):
        k_cross(s).wait_recv()

        @pl.when(has_to)
        def _():
            k_far(s).start()
        in_range(s, 0, n_a, lambda s: start_frames(s, PART))

    def pass_far(s):
        @pl.when(has_from)
        def _():
            k_far(s).wait_recv()
        in_range(s, 0, n_a, lambda s: start_frames(s, FAR))

    def frames_in(s, row_list):
        for row in row_list:
            each_side(lambda side: k_frame_in(s, side, row).wait_recv(), row_exists(row))

    def frames_out(s, row_list):
        for row in row_list:
            each_side(lambda side: g_frame(s, side, row).start(), row_exists(row))

    def compute_a(s):
        frames_in(s, range(3))
        attend(s, (1, 9))
        frames_out(s, (FAR, PART, OWN))

    def compute_b(s):
        attend(s, (1, 3))

    def compute_c(s):
        frames_in(s, [OWN])
        attend(s, (3, 3))
        frames_out(s, [OWN])

    def add_frames(s, row):
        def add(side):
            g_frame_in(s, side, row).wait_recv()
            ga[s, row] = ga[s, row] + gf[s, side, row].astype(jnp.float32)
        each_side(add, row_exists(row))

    def reduce_far(s):
        in_range(s, 0, n_a, lambda s: add_frames(s, FAR))

        @pl.when(has_from)
        def _():
            gp[s, FAR] = ga[s, FAR].astype(jnp.bfloat16)
            g_far(s).start()

    def reduce_partner(s):
        in_range(s, 0, n_a, lambda s: add_frames(s, PART))

        @pl.when(has_to)
        def _():
            g_far(s).wait_recv()
            ga[s, PART] = ga[s, PART] + gy[s].astype(jnp.float32)
        gp[s, PART] = ga[s, PART].astype(jnp.bfloat16)
        g_cross(s).start()

    def finish(s):
        in_range(s, 0, n_a, lambda s: add_frames(s, OWN))
        in_range(s, n_rows, heads, lambda s: add_frames(s, OWN))
        if n_rows:
            @pl.when(s < n_rows)
            def _():
                g_cross(s).wait_recv()
                ga[s, OWN] = ga[s, OWN] + gz[s].astype(jnp.float32)
        grad = ga[s, OWN].astype(jnp.bfloat16)
        vgs[s] = grad
        up_s[s] = dot(hid_t[...], grad, 1, 0)
        back[...] = back[...] + dot(grad, ui_wide[meta[0, s]], 1, 1)

    for s in range(min(AHEAD, n_rows)):
        k_cross(s).start()

    @pl.loop(0, heads)
    def _(s):
        in_range(s, 0, n_a, lambda s: start_frames(s, OWN))
        in_range(s, n_rows, heads, lambda s: start_frames(s, OWN))

    depth = clean_ref.shape[1]
    rank = ui_ref.shape[0]
    copies = LANES // rank
    per = heads
    lane8 = lax.broadcasted_iota(jnp.int32, (1, copies, LANES), 2)
    row8 = lax.broadcasted_iota(jnp.int32, (1, copies, LANES), 1)
    pick = lane8 // rank == row8

    block = 512
    blocks = depth // block
    sketch_rows = SKETCH // LANES
    pieces = flat.shape[0] // sketch_rows

    def place_down(base, n, wide):
        kept = jnp.where(pick, wide.reshape(-1, copies, LANES), 0.0)
        flat[pl.ds(pl.multiple_of(base + n * (block // copies), 64), block // copies), :] = jnp.sum(kept, axis=1)

    def place_up(base, m, grad):
        for r in range(rank):
            flat[pl.ds(base + r * per + m, 1), :] = grad[r:r + 1, :]

    for n, ref in enumerate((q_ref, c_ref, tk_ref)):
        loads[n].wait()

        @pl.loop(0, heads)
        def _(j):
            by_head[n + 1, j] = ref[:, columns(j)]

    @pl.loop(0, heads)
    def _(j):
        ui_wide[j] = jnp.concatenate([ui_ref[:, columns(j)]] * copies, axis=0)

    back[...] = jnp.zeros_like(back)
    for n in range(3, 6):
        loads[n].wait()
    level = jnp.full((1, block), time_ref[0], jnp.int32).astype(jnp.float32) / 1000.0

    def mix(n, hid):
        cols = columns(n, block)
        mixed = (
            (1.0 - level) * clean_ref[:, cols].astype(jnp.float32)
            + level * noise_ref[:, cols].astype(jnp.float32)
        ).astype(jnp.bfloat16)
        mixed_t[n] = jnp.transpose(mixed)
        return hid + dot(di_ref[:, cols], mixed, 1, 1)

    hid_t[...] = lax.fori_loop(0, blocks, mix, jnp.zeros((rank, tile), jnp.float32)).astype(jnp.bfloat16)
    text_hid[...] = dot(dt_ref[...], text_ref[...], 1, 1)

    @pl.loop(0, pieces)
    def _(m):
        pos = lax.broadcasted_iota(jnp.int32, (sketch_rows, LANES), 0) * LANES
        pos = pos + lax.broadcasted_iota(jnp.int32, (sketch_rows, LANES), 1) + m * SKETCH
        bits = pos * 1103515245 + seed_ref[0] * 12345 + 1013904223
        bits = bits ^ (bits >> 16)
        bits = bits * 73244475
        bits = bits ^ (bits >> 16)
        signs[m] = (1 - 2 * ((bits >> 7) & 1)).astype(jnp.float32)

    def text_grads():
        th_hi, th_lo = split2(text_hid[...])

        def per_head(j, text_back):
            tv_hi, tv_lo = split2(tvs[meta[1, j]])
            place_up(960, j, dot(th_hi, tv_hi, 1, 0) + (dot(th_hi, tv_lo, 1, 0) + dot(th_lo, tv_hi, 1, 0)))
            cols = jnp.concatenate([ut_ref[:, columns(j)]] * copies, axis=0)
            return text_back + (dot(tv_hi, cols, 1, 1) + dot(tv_lo, cols, 1, 1))

        text_back = lax.fori_loop(0, heads, per_head, jnp.zeros((tile, LANES), jnp.float32))
        tb_hi, tb_lo = split2(text_back)

        @pl.loop(0, blocks)
        def _(n):
            text = text_ref[:, columns(n, block)]
            place_down(576, n, dot(text, tb_hi, 0, 0) + dot(text, tb_lo, 0, 0))

    @pl.loop(0, heads + 6)
    def _(i):
        in_range(i + AHEAD, 0, n_rows, lambda s: k_cross(s).start())
        in_range(i, 0, n_rows, pass_partner)
        in_range(i - 1, 0, n_rows, pass_far)
        in_range(i - 2, 0, n_a, compute_a)
        in_range(i - 2, n_a, n_rows, compute_b)
        in_range(i - 2, n_rows, heads, compute_c)
        in_range(i - 3, 0, n_rows, reduce_far)
        in_range(i - 4, 0, n_rows, reduce_partner)
        in_range(i, heads + 2, heads + 3, lambda i: text_grads())
        in_range(i - 6, 0, heads, finish)

    @pl.loop(0, heads)
    def _(j):
        slot = meta[1, j]
        vg_ref[:, columns(j)] = vgs[slot]
        place_up(384, j, up_s[slot])

    low_back = back[...].astype(jnp.bfloat16)

    @pl.loop(0, blocks)
    def _(n):
        place_down(0, n, dot(mixed_t[n], low_back, 1, 0))

    acc = flat[0:sketch_rows] * signs[0]
    for m in range(1, pieces):
        acc = acc + flat[m * sketch_rows:(m + 1) * sketch_rows] * signs[m]
    part[...] = (acc * (token_total * pieces) ** -0.5).reshape(count, sketch_rows // count, LANES)

    def send1(k):
        i = lax.rem(g + k, count)
        return remote(part.at[i], box1.at[g], a_s.at[0, k], a_r.at[0, g], in_ring(i))

    def send2(k):
        i = lax.rem(w + k, count)
        return remote(box2.at[w], box2.at[w], a_s.at[1, k], a_r.at[1, w], in_plane(i))

    def send3(k):
        i = lax.rem(g + k, count)
        return remote(out_ref.at[g], out_ref.at[g], a_s.at[2, k], a_r.at[2, g], in_ring(i))

    def recv(phase, dst, i):
        return remote(dst.at[i], dst.at[i], a_s.at[phase, 0], a_r.at[phase, i], in_ring(lax.rem(g + 1, count)))

    def phase(n, me, dst, send):
        @pl.loop(1, count)
        def _(k):
            send(k).start()

        @pl.loop(1, count)
        def _(k):
            recv(n, dst, lax.rem(me + k, count)).wait_recv()

    box1[g] = part[g]
    phase(0, g, box1, send1)
    box2[w] = jnp.sum(box1[...], axis=0)
    phase(1, w, box2, send2)
    out_ref[g] = jnp.sum(box2[...], axis=0)
    phase(2, g, out_ref, send3)

    @pl.loop(1, count)
    def _(k):
        send1(k).wait_send()
        send2(k).wait_send()
        send3(k).wait_send()

    @pl.loop(0, heads)
    def _(s):
        def sent_rows(s):
            k_cross(s).wait_send()
            g_cross(s).wait_send()

            @pl.when(has_to)
            def _():
                k_far(s).wait_send()

            @pl.when(has_from)
            def _():
                g_far(s).wait_send()

        def sent_frames(s, row_list):
            for row in row_list:
                each_side(lambda side: k_frame(s, side, row).wait_send(), row_exists(row))
                each_side(lambda side: g_frame(s, side, row).wait_send(), row_exists(row))
        in_range(s, 0, n_rows, sent_rows)
        in_range(s, 0, n_a, lambda s: sent_frames(s, range(3)))
        in_range(s, n_rows, heads, lambda s: sent_frames(s, [OWN]))


def attention(n_a, n_b, cid, frames, rows, *args):
    tile, width = args[4].shape
    depth = args[12].shape[1]
    rank = args[5].shape[0]
    lines = SKETCH // LANES
    heads = width // LANES
    vmem = pl.BlockSpec(memory_space=pltpu.VMEM)
    sem = pltpu.SemaphoreType.DMA
    bf, f32 = jnp.bfloat16, jnp.float32
    box = (tile, LANES)
    return pl.pallas_call(
        functools.partial(attention_kernel, n_a, n_b, heads, frames, rows, tile * frames * rows),
        out_shape=(jax.ShapeDtypeStruct((tile, width), bf), jax.ShapeDtypeStruct((16, lines // 16, LANES), f32)),
        in_specs=[pl.BlockSpec(memory_space=pltpu.SMEM)] * 4 + [vmem] * 5 + [pl.BlockSpec(memory_space=pl.ANY)] * 6,
        out_specs=(vmem, vmem),
        scratch_shapes=[
            pltpu.VMEM((tile, width), bf), pltpu.VMEM((tile, width), bf), pltpu.VMEM((tile, width), bf),
            pltpu.VMEM((tile, depth), bf), pltpu.VMEM((tile, depth), bf), pltpu.VMEM((tile, depth), bf),
            sem((6,)),
            pltpu.VMEM((depth // 512, 512, tile), bf),
            pltpu.VMEM((rank, tile), bf),
            pltpu.VMEM((rank, tile), f32),
            pltpu.VMEM((heads, LANES, LANES), bf),
            pltpu.VMEM((tile, LANES), f32),
            pltpu.VMEM((heads, rank, LANES), f32),
            pltpu.VMEM((9 * lines, LANES), f32),
            pltpu.VMEM((9, lines, LANES), f32),
            pltpu.VMEM((16, lines // 16, LANES), f32),
            pltpu.VMEM((16, lines // 16, LANES), f32),
            pltpu.VMEM((16, lines // 16, LANES), f32),
            sem((3, 16)), sem((3, 16)),
            pltpu.VMEM((4, heads) + box, bf),
            pltpu.VMEM((heads, 9) + box, bf),
            pltpu.VMEM((heads, 9) + box, bf),
            pltpu.VMEM((heads, 3) + box, f32),
            pltpu.VMEM((heads, 2, 3) + box, bf),
            pltpu.VMEM((heads,) + box, bf),
            pltpu.VMEM((heads,) + box, bf),
            pltpu.VMEM((heads,) + box, bf),
            pltpu.VMEM((heads,) + box, f32),
            pltpu.VMEM((10, tile, tile), f32),
            pltpu.VMEM((10, tile, tile), bf),
            sem((heads,)), sem((heads,)), sem((heads,)), sem((heads,)),
            sem((heads, 2, 3)), sem((heads, 2, 3)), sem((heads, 2, 3)), sem((heads, 2, 3)),
            sem((heads,)), sem((heads,)), sem((heads,)), sem((heads,)),
        ],
        compiler_params=pltpu.CompilerParams(
            collective_id=cid, has_side_effects=True, vmem_limit_bytes=56 << 20
        ),
    )(*args)


def split2(x):
    hi = x.astype(jnp.bfloat16)
    return hi, (x - hi.astype(jnp.float32)).astype(jnp.bfloat16)


VARIANTS = ((2, 3), (3, 3), (4, 3), (5, 3), (7, 2), (12, 0))


def plan_kernel(variants, heads, radii, choice, meta, closed):
    kinds = []
    counts = [jnp.int32(0)] * 4
    ranks = []
    for j in range(heads):
        far_f, far_r = radii[j, 0] > 0, radii[j, 1] > 0
        kind = jnp.where(far_r, jnp.where(far_f, 0, 1), jnp.where(far_f, 2, 3))
        kinds.append(kind)
        rank = jnp.int32(0)
        for t in range(4):
            rank = jnp.where(kind == t, counts[t], rank)
            counts[t] = counts[t] + jnp.where(kind == t, 1, 0)
        ranks.append(rank)
    pick = jnp.int32(len(variants) - 1)
    a, b = jnp.int32(variants[-1][0]), jnp.int32(variants[-1][1])
    for i in reversed(range(len(variants) - 1)):
        va, vb = variants[i]
        vc = heads - va - vb
        fits = (counts[0] <= va) & (counts[0] + counts[1] <= va + vb) & (counts[0] + counts[2] <= va + vc)
        pick = jnp.where(fits, i, pick)
        a, b = jnp.where(fits, va, a), jnp.where(fits, vb, b)
    c = heads - a - b
    over_b = jnp.maximum(counts[1] - b, 0)
    over_c = jnp.maximum(counts[2] - c, 0)
    spare_a = a - counts[0] - over_b - over_c
    spare_b = b - (counts[1] - over_b)
    choice[0] = pick
    for j in range(heads):
        kind, rank = kinds[j], ranks[j]
        slot_b = jnp.where(rank < over_b, counts[0] + rank, a + rank - over_b)
        slot_c = jnp.where(rank < over_c, counts[0] + over_b + rank, heads - counts[2] + rank)
        left = rank - spare_a - spare_b
        slot_d = jnp.where(
            rank < spare_a,
            counts[0] + over_b + over_c + rank,
            a + b + left,
        )
        slot = jnp.where(kind == 0, rank, jnp.where(kind == 1, slot_b, jnp.where(kind == 2, slot_c, slot_d)))
        meta[0, slot] = j
        meta[1, j] = slot
        for r in range(3):
            closed[r, slot] = jnp.where(radii[j, r] > 0, 0.0, NEG)


def plan(radii):
    heads = radii.shape[0]
    smem = pl.BlockSpec(memory_space=pltpu.SMEM)
    return pl.pallas_call(
        functools.partial(plan_kernel, VARIANTS, heads),
        out_shape=(
            jax.ShapeDtypeStruct((1,), jnp.int32),
            jax.ShapeDtypeStruct((2, heads), jnp.int32),
            jax.ShapeDtypeStruct((3, heads), jnp.float32),
        ),
        in_specs=[smem],
        out_specs=(smem, smem, smem),
    )(radii)


def per_device(
    clean_latents, gaussian_noise, text_states, queries, key_states, cotangent, text_keys,
    window_radii, timestep, sketch_seed, down_image, up_image, down_text, up_text,
):
    width = queries.shape[-1]
    depth = clean_latents.shape[-1]
    frames, rows = lax.axis_size("tm"), lax.axis_size("height")
    choice, meta, closed = plan(window_radii)
    branches = [
        functools.partial(attention, a, b, i + 1, frames, rows) for i, (a, b) in enumerate(VARIANTS)
    ]
    operands = (
        meta, closed, timestep, sketch_seed,
        key_states.reshape(-1, width), up_image, up_text, down_image.T, down_text.T,
        queries.reshape(-1, width), cotangent.reshape(-1, width), text_keys,
        clean_latents.reshape(-1, depth), gaussian_noise.reshape(-1, depth), text_states,
    )
    if len(branches) == 1:
        vg, sk = branches[0](*operands)
    else:
        vg, sk = lax.switch(choice[0], branches, *operands)
    return vg.reshape(queries.shape), sk.reshape(-1)


def solution(mesh):
    block = P("tm", "height", None, None)
    return jax.shard_map(
        per_device,
        mesh=mesh,
        in_specs=(block, block, P(), block, block, block) + (P(),) * 8,
        out_specs=(block, P()),
        check_vma=False,
    )
```

time: 124 us -> 122 us (0.984)
  loops' own time: 0.05 us -> 5.31 us
  Pallas kernels: 117 us -> 112 us
  between operations: 2.6 us -> 1.3 us
    pallas_call x1 -> x0, Pallas kernels: 29.3 us -> none  [sketch(): pl.pallas_call(functools.partial(sketch_kernel, token_total), out_shape=j...]
    pallas_call x1, Pallas kernels: 86.1 us -> 110 us  [attention(): pl.pallas_call(functools.partial(attention_kernel, n_a, n_b, heads, frame...]
    another operation x1, loops' own time: 0.05 us -> 5.31 us  [per_device(): vg, sk = lax.switch(choice[0], branches, *operands)]
    unnamed x4 -> x3, local copies, waits for them, and re-layouts: 2.84 us -> 2.88 us
where the time goes in v3:
time: 122 us; the launch traced here: 121 us
  Pallas kernels  112 us (92%)
  loops' own time  5.31 us (4%)
  local copies, waits for them, and re-layouts  2.88 us (2%)
  between operations  1.3 us (1%)
    pallas_call x1, Pallas kernels, attention(): pl.pallas_call(functools.partial(attention_kernel, n_a, n_b, heads, frame...  110 us
    another operation x1, loops' own time, per_device(): vg, sk = lax.switch(choice[0], branches, *operands)  5.31 us
    unnamed x3, local copies, waits for them, and re-layouts  2.88 us

profile of v3, /device:TPU:1, one launch (start us, length us, event | category | flops | bytes accessed | tf_op | source)
XLA Modules:
  0.0 121.4 jit_solution(11328174263586697915)
XLA Ops:
  0.6 1.4 %copy.16.radii = s32[12,3]{1,0:T(8,128)} copy(s32[12,3]{0,1:T(4,128)} %param.27) | data formatting | bytes 288 | tf_op args[7]
  2.0 1.7 %shard_map.149 = (s32[1]{0:T(128)}, s32[2,12]{1,0:T(2,128)S(1)}, f32[3,12]{1,0:T(4,128)S(1)}) custom-call(s32[12,3]{1,0:T(8,128)} %copy.16.radii), custom_call_target="tpu_custom_call" | custom-call | tf_op jit(solution)/shard_map/pallas_call | solution.py:576
  4.4 115.5 %conditional.1 = ((bf16[256,1536]{1,0:T(8,128)(2,1)S(1)}, f32[16,8,128]{2,1,0:T(8,128)S(1)})) conditional(s32[]{:T(128)} %bitcast, (s32[2,12]{1,0:T(2,128)S(1)}, f32[3,12]{1,0:T(4,128)S(1)}, s32[1]{0:T(128)}, s32[1]{0:T(128)}, bf16[256,1536]{1,0:T(8,128)(2,1)}, /*index=5*/bf16[16,1536]{1,0:T(8,128)(2,1)}, ...), branch_computations={%region_0.0_spmd, %region_1.0_spmd, %region_2.0_spmd, %region_3.0_... | conditional | bytes 8 | solution.py:608
  9.1 110.2 %branch_2_fun.1 = (bf16[256,1536]{1,0:T(8,128)(2,1)S(1)}, f32[16,8,128]{2,1,0:T(8,128)S(1)}) custom-call(s32[2,12]{1,0:T(2,128)S(1)} %get-tuple-element.228.meta, f32[3,12]{1,0:T(4,128)S(1)} %get-tuple-element.229.closed, s32[1]{0:T(128)} %get-tuple-element.230.time_ref, s32[1]{0:T(128)} %get-tuple-element.231.seed_ref, ...), custom_call_target="tpu_custom_call" | custom-call | tf_op jit(solution)/shard_map/cond/branch_2_fun/pallas_call | solution.py:479
  119.9 0.9 copy.31
  120.8 0.6 copy.32

commit v4 on v3

--- a/solution.py
+++ b/solution.py
@@ -14,7 +14,7 @@
 NEG = -1e30
 LOG2E = 1.4426950408889634
 OWN, PART, FAR = 0, 1, 2
-AHEAD = 3
+AHEAD = 1
 
 
 def dot(a, b, ca, cb):
@@ -52,6 +52,15 @@
     low = (jnp.maximum(f - 1, 0), h)
     high = (jnp.minimum(f + 1, frames - 1), h)
     sides = ((low, has_low), (high, has_high))
+    odd = lax.rem(f, 2)
+    has_outer = jnp.where(odd == 1, f < frames - 1, f > 0)
+    outer_f = jnp.where(has_outer, f - 1 + 2 * odd, f)
+    outer = (outer_f, h)
+    across = (outer_f, partner[1])
+    inner = (f + 1 - 2 * odd, h)
+    outer_side, inner_side = odd, 1 - odd
+    outer_tile = 3 * (1 + odd)
+    inner_tile = 3 * (2 - odd)
 
     g = 2 * f + lax.rem(h, 2)
     w = h // 2
@@ -111,31 +120,69 @@
     def k_cross(s):
         return remote(kr.at[s, OWN], kr.at[s, PART], kz_s.at[s], kz_r.at[s], partner)
 
+    def k_across(s):
+        target = jnp.where(has_outer, inner_tile, 0) + PART
+        return remote(kr.at[s, OWN], kr.at[s, target], kz_s.at[s], kz_r.at[s], across)
+
+    def k_relay(s):
+        return remote(
+            kr.at[s, outer_tile + PART], kr.at[s, PART],
+            kf_s.at[s, outer_side, PART], kf_r.at[s, 1 - outer_side, PART], outer,
+        )
+
     def k_far(s):
         return remote(kr.at[s, PART], kr.at[s, FAR], ky_s.at[s], ky_r.at[s], far_to)
 
-    def k_frame(s, side, row):
-        return remote(
-            kr.at[s, row], kr.at[s, 3 * (2 - side) + row],
-            kf_s.at[s, side, row], kf_r.at[s, 1 - side, row], sides[side][0],
-        )
-
-    def k_frame_in(s, side, row):
-        return remote(
-            kr.at[s, row], kr.at[s, 3 * (1 + side) + row],
-            kf_s.at[s, side, row], kf_r.at[s, side, row], sides[side][0],
-        )
-
-    def g_frame(s, side, row):
-        return remote(
-            gp.at[s, 3 * (1 + side) + row], gf.at[s, 1 - side, row],
-            gf_s.at[s, side, row], gf_r.at[s, 1 - side, row], sides[side][0],
-        )
-
-    def g_frame_in(s, side, row):
-        return remote(
-            gp.at[s, 3 * (1 + side) + row], gf.at[s, side, row],
-            gf_s.at[s, side, row], gf_r.at[s, side, row], sides[side][0],
+    def k_far_outer(s):
+        return remote(
+            kr.at[s, outer_tile + PART], kr.at[s, outer_tile + FAR],
+            kf_s.at[s, outer_side, FAR], kf_r.at[s, outer_side, FAR], far_to,
+        )
+
+    def k_inner(s, row):
+        return remote(
+            kr.at[s, row], kr.at[s, outer_tile + row],
+            kf_s.at[s, inner_side, row], kf_r.at[s, 1 - inner_side, row], inner,
+        )
+
+    def k_frame(s, side):
+        return remote(
+            kr.at[s, OWN], kr.at[s, 3 * (2 - side)],
+            kf_s.at[s, side, OWN], kf_r.at[s, 1 - side, OWN], sides[side][0],
+        )
+
+    def k_in(s, tile_index, side, row):
+        return remote(
+            kr.at[s, tile_index], kr.at[s, tile_index], kf_s.at[s, side, row], kf_r.at[s, side, row], inner,
+        )
+
+    def g_frame(s, side):
+        return remote(
+            gp.at[s, 3 * (1 + side)], gf.at[s, 1 - side, OWN],
+            gf_s.at[s, side, OWN], gf_r.at[s, 1 - side, OWN], sides[side][0],
+        )
+
+    def g_inner(s, row):
+        return remote(
+            gp.at[s, inner_tile + row], gf.at[s, 1 - inner_side, row],
+            gf_s.at[s, inner_side, row], gf_r.at[s, 1 - inner_side, row], inner,
+        )
+
+    def g_far_outer(s):
+        return remote(
+            gp.at[s, outer_tile + FAR], gf.at[s, outer_side, FAR],
+            gf_s.at[s, outer_side, FAR], gf_r.at[s, outer_side, FAR], far_from,
+        )
+
+    def g_relay(s):
+        return remote(
+            gp.at[s, PART], gf.at[s, 1 - outer_side, PART],
+            gf_s.at[s, outer_side, PART], gf_r.at[s, 1 - outer_side, PART], outer,
+        )
+
+    def g_in(s, side, row):
+        return remote(
+            gf.at[s, side, row], gf.at[s, side, row], gf_s.at[s, side, row], gf_r.at[s, side, row], inner,
         )
 
     def g_far(s):
@@ -144,16 +191,19 @@
     def g_cross(s):
         return remote(gp.at[s, PART], gz.at[s], gz_s.at[s], gz_r.at[s], partner)
 
-    def each_side(fn, extra=None):
+    def g_across(s):
+        return remote(gp.at[s, outer_tile + PART], gz.at[s], gz_s.at[s], gz_r.at[s], across)
+
+    def each_side(fn):
         for side in range(2):
-            cond = sides[side][1] if extra is None else sides[side][1] & extra
-
-            @pl.when(cond)
+            @pl.when(sides[side][1])
             def _(side=side):
                 fn(side)
 
-    def row_exists(row):
-        return has_from if row == FAR else None
+    def when(cond, fn):
+        @pl.when(cond)
+        def _():
+            fn()
 
     lane = lax.broadcasted_iota(jnp.int32, (2, 8, tile), 2)
     group = lax.broadcasted_iota(jnp.int32, (2, 8, tile), 0)
@@ -217,71 +267,105 @@
             def _():
                 fn(i)
 
-    def start_frames(s, row):
-        each_side(lambda side: k_frame(s, side, row).start(), row_exists(row))
+    def start_cross(s):
+        in_range(s, 0, n_a, lambda s: k_across(s).start())
+        in_range(s, n_a, n_rows, lambda s: k_cross(s).start())
+
+    def start_frames(s):
+        each_side(lambda side: k_frame(s, side).start())
+
+    def pass_outer(s):
+        k_cross(s).wait_recv()
+
+        @pl.when(has_outer)
+        def _():
+            k_relay(s).start()
+            when(has_to, lambda: k_far_outer(s).start())
 
     def pass_partner(s):
+        when(has_outer, lambda: k_in(s, PART, outer_side, PART).wait_recv())
+        when(has_to, lambda: k_far(s).start())
+        k_inner(s, PART).start()
+
+    def pass_partner_b(s):
         k_cross(s).wait_recv()
-
-        @pl.when(has_to)
-        def _():
-            k_far(s).start()
-        in_range(s, 0, n_a, lambda s: start_frames(s, PART))
+        when(has_to, lambda: k_far(s).start())
 
     def pass_far(s):
         @pl.when(has_from)
         def _():
             k_far(s).wait_recv()
-        in_range(s, 0, n_a, lambda s: start_frames(s, FAR))
-
-    def frames_in(s, row_list):
-        for row in row_list:
-            each_side(lambda side: k_frame_in(s, side, row).wait_recv(), row_exists(row))
-
-    def frames_out(s, row_list):
-        for row in row_list:
-            each_side(lambda side: g_frame(s, side, row).start(), row_exists(row))
+            in_range(s, 0, n_a, lambda s: k_inner(s, FAR).start())
+
+    def frames_in(s):
+        each_side(lambda side: k_in(s, 3 * (1 + side), side, OWN).wait_recv())
 
     def compute_a(s):
-        frames_in(s, range(3))
+        frames_in(s)
+        k_in(s, inner_tile + PART, inner_side, PART).wait_recv()
+
+        @pl.when(has_from)
+        def _():
+            k_in(s, inner_tile + FAR, inner_side, FAR).wait_recv()
+            when(has_outer, lambda: k_in(s, outer_tile + FAR, outer_side, FAR).wait_recv())
         attend(s, (1, 9))
-        frames_out(s, (FAR, PART, OWN))
+
+        @pl.when(has_from)
+        def _():
+            when(has_outer, lambda: g_far_outer(s).start())
+            g_inner(s, FAR).start()
+        g_inner(s, PART).start()
+        each_side(lambda side: g_frame(s, side).start())
 
     def compute_b(s):
         attend(s, (1, 3))
 
     def compute_c(s):
-        frames_in(s, [OWN])
+        frames_in(s)
         attend(s, (3, 3))
-        frames_out(s, [OWN])
-
-    def add_frames(s, row):
-        def add(side):
-            g_frame_in(s, side, row).wait_recv()
-            ga[s, row] = ga[s, row] + gf[s, side, row].astype(jnp.float32)
-        each_side(add, row_exists(row))
+        each_side(lambda side: g_frame(s, side).start())
+
+    def add_in(s, side, row, into):
+        g_in(s, side, row).wait_recv()
+        ga[s, into] = ga[s, into] + gf[s, side, row].astype(jnp.float32)
+
+    def add_frames(s):
+        each_side(lambda side: add_in(s, side, OWN, OWN))
 
     def reduce_far(s):
-        in_range(s, 0, n_a, lambda s: add_frames(s, FAR))
-
         @pl.when(has_from)
         def _():
+            in_range(s, 0, n_a, lambda s: add_in(s, inner_side, FAR, FAR))
             gp[s, FAR] = ga[s, FAR].astype(jnp.bfloat16)
             g_far(s).start()
 
     def reduce_partner(s):
-        in_range(s, 0, n_a, lambda s: add_frames(s, PART))
+        in_range(s, 0, n_a, lambda s: add_in(s, inner_side, PART, PART))
 
         @pl.when(has_to)
         def _():
             g_far(s).wait_recv()
             ga[s, PART] = ga[s, PART] + gy[s].astype(jnp.float32)
         gp[s, PART] = ga[s, PART].astype(jnp.bfloat16)
-        g_cross(s).start()
+
+        def send_a(s):
+            when(has_outer, lambda: g_relay(s).start())
+            when(jnp.logical_not(has_outer), lambda: g_cross(s).start())
+        in_range(s, 0, n_a, send_a)
+        in_range(s, n_a, n_rows, lambda s: g_cross(s).start())
+
+    def relay(s):
+        @pl.when(has_outer)
+        def _():
+            g_in(s, outer_side, PART).wait_recv()
+            ga[s, FAR] = gp[s, outer_tile + PART].astype(jnp.float32) + gf[s, outer_side, PART].astype(jnp.float32)
+            when(has_to, lambda: add_in(s, outer_side, FAR, FAR))
+            gp[s, outer_tile + PART] = ga[s, FAR].astype(jnp.bfloat16)
+            g_across(s).start()
 
     def finish(s):
-        in_range(s, 0, n_a, lambda s: add_frames(s, OWN))
-        in_range(s, n_rows, heads, lambda s: add_frames(s, OWN))
+        in_range(s, 0, n_a, add_frames)
+        in_range(s, n_rows, heads, add_frames)
         if n_rows:
             @pl.when(s < n_rows)
             def _():
@@ -292,13 +376,13 @@
         up_s[s] = dot(hid_t[...], grad, 1, 0)
         back[...] = back[...] + dot(grad, ui_wide[meta[0, s]], 1, 1)
 
-    for s in range(min(AHEAD, n_rows)):
-        k_cross(s).start()
+    for s in map(jnp.int32, range(min(AHEAD, n_rows))):
+        start_cross(s)
 
     @pl.loop(0, heads)
     def _(s):
-        in_range(s, 0, n_a, lambda s: start_frames(s, OWN))
-        in_range(s, n_rows, heads, lambda s: start_frames(s, OWN))
+        in_range(s, 0, n_a, start_frames)
+        in_range(s, n_rows, heads, start_frames)
 
     depth = clean_ref.shape[1]
     rank = ui_ref.shape[0]
@@ -376,18 +460,21 @@
             text = text_ref[:, columns(n, block)]
             place_down(576, n, dot(text, tb_hi, 0, 0) + dot(text, tb_lo, 0, 0))
 
-    @pl.loop(0, heads + 6)
+    @pl.loop(0, heads + 8)
     def _(i):
-        in_range(i + AHEAD, 0, n_rows, lambda s: k_cross(s).start())
-        in_range(i, 0, n_rows, pass_partner)
-        in_range(i - 1, 0, n_rows, pass_far)
-        in_range(i - 2, 0, n_a, compute_a)
-        in_range(i - 2, n_a, n_rows, compute_b)
-        in_range(i - 2, n_rows, heads, compute_c)
-        in_range(i - 3, 0, n_rows, reduce_far)
-        in_range(i - 4, 0, n_rows, reduce_partner)
-        in_range(i, heads + 2, heads + 3, lambda i: text_grads())
-        in_range(i - 6, 0, heads, finish)
+        in_range(i + AHEAD, 0, n_rows, start_cross)
+        in_range(i - 8, 0, heads, finish)
+        in_range(i, heads + 3, heads + 4, lambda i: text_grads())
+        in_range(i - 6, 0, n_a, relay)
+        in_range(i - 5, 0, n_rows, reduce_partner)
+        in_range(i - 4, 0, n_rows, reduce_far)
+        in_range(i - 3, n_rows, heads, compute_c)
+        in_range(i - 3, n_a, n_rows, compute_b)
+        in_range(i - 3, 0, n_a, compute_a)
+        in_range(i - 2, 0, n_rows, pass_far)
+        in_range(i - 1, 0, n_a, pass_partner)
+        in_range(i, n_a, n_rows, pass_partner_b)
+        in_range(i, 0, n_a, pass_outer)
 
     @pl.loop(0, heads)
     def _(j):
@@ -448,22 +535,33 @@
         def sent_rows(s):
             k_cross(s).wait_send()
             g_cross(s).wait_send()
-
-            @pl.when(has_to)
-            def _():
-                k_far(s).wait_send()
+            when(has_to, lambda: k_far(s).wait_send())
+            when(has_from, lambda: g_far(s).wait_send())
+
+        def sent_own(s):
+            each_side(lambda side: k_frame(s, side).wait_send())
+            each_side(lambda side: g_frame(s, side).wait_send())
+
+        def sent_a(s):
+            sent_own(s)
+            k_inner(s, PART).wait_send()
+            g_inner(s, PART).wait_send()
 
             @pl.when(has_from)
             def _():
-                g_far(s).wait_send()
-
-        def sent_frames(s, row_list):
-            for row in row_list:
-                each_side(lambda side: k_frame(s, side, row).wait_send(), row_exists(row))
-                each_side(lambda side: g_frame(s, side, row).wait_send(), row_exists(row))
+                k_inner(s, FAR).wait_send()
+                g_inner(s, FAR).wait_send()
+                when(has_outer, lambda: g_far_outer(s).wait_send())
+
+            @pl.when(has_outer)
+            def _():
+                k_relay(s).wait_send()
+                g_relay(s).wait_send()
+                when(has_to, lambda: k_far_outer(s).wait_send())
+
         in_range(s, 0, n_rows, sent_rows)
-        in_range(s, 0, n_a, lambda s: sent_frames(s, range(3)))
-        in_range(s, n_rows, heads, lambda s: sent_frames(s, [OWN]))
+        in_range(s, 0, n_a, sent_a)
+        in_range(s, n_rows, heads, sent_own)
 
 
 def attention(n_a, n_b, cid, frames, rows, *args):
@@ -523,7 +621,7 @@
     return hi, (x - hi.astype(jnp.float32)).astype(jnp.bfloat16)
 
 
-VARIANTS = ((2, 3), (3, 3), (4, 3), (5, 3), (7, 2), (12, 0))
+VARIANTS = ((2, 2), (3, 2), (4, 2), (5, 2), (6, 3), (12, 0))
 
 
 def plan_kernel(variants, heads, radii, choice, meta, closed):
@@ -531,7 +629,7 @@
     counts = [jnp.int32(0)] * 4
     ranks = []
     for j in range(heads):
-        far_f, far_r = radii[j, 0] > 0, radii[j, 1] > 0
+        far_f, far_r = radii[0, j] > 0, radii[1, j] > 0
         kind = jnp.where(far_r, jnp.where(far_f, 0, 1), jnp.where(far_f, 2, 3))
         kinds.append(kind)
         rank = jnp.int32(0)
@@ -567,11 +665,11 @@
         meta[0, slot] = j
         meta[1, j] = slot
         for r in range(3):
-            closed[r, slot] = jnp.where(radii[j, r] > 0, 0.0, NEG)
+            closed[r, slot] = jnp.where(radii[r, j] > 0, 0.0, NEG)
 
 
 def plan(radii):
-    heads = radii.shape[0]
+    heads = radii.shape[1]
     smem = pl.BlockSpec(memory_space=pltpu.SMEM)
     return pl.pallas_call(
         functools.partial(plan_kernel, VARIANTS, heads),
@@ -592,7 +690,7 @@
     width = queries.shape[-1]
     depth = clean_latents.shape[-1]
     frames, rows = lax.axis_size("tm"), lax.axis_size("height")
-    choice, meta, closed = plan(window_radii)
+    choice, meta, closed = plan(window_radii.T)
     branches = [
         functools.partial(attention, a, b, i + 1, frames, rows) for i, (a, b) in enumerate(VARIANTS)
     ]

time: 122 us -> 104 us (0.85)
  Pallas kernels: 112 us -> 99.9 us
  loops' own time: 5.31 us -> 0.86 us
  local copies, waits for them, and re-layouts: 2.88 us -> 1.52 us
    pallas_call x1, Pallas kernels: 110 us -> 98.3 us  [attention(): pl.pallas_call(functools.partial(attention_kernel, n_a, n_b, heads, frame...]
    another operation x1, loops' own time: 5.31 us -> 0.86 us  [per_device(): vg, sk = lax.switch(choice[0], branches, *operands)]
    unnamed x3 -> x2, local copies, waits for them, and re-layouts: 2.88 us -> 1.52 us
where the time goes in v4:
time: 104 us
  Pallas kernels  99.9 us (96%)
  local copies, waits for them, and re-layouts  1.52 us (1%)
  between operations  1.3 us (1%)
    pallas_call x1, Pallas kernels, attention(): pl.pallas_call(functools.partial(attention_kernel, n_a, n_b, heads, frame...  98.3 us

profile of v4, /device:TPU:1, one launch (start us, length us, event | category | flops | bytes accessed | tf_op | source)
XLA Modules:
  0.0 103.6 jit_solution(17079420377934177614)
XLA Ops:
  0.6 1.6 %shard_map.149 = (s32[1]{0:T(128)}, s32[2,12]{1,0:T(2,128)S(1)}, f32[3,12]{1,0:T(4,128)S(1)}) custom-call(s32[3,12]{1,0:T(4,128)} %bitcast.55), custom_call_target="tpu_custom_call" | custom-call | tf_op jit(solution)/shard_map/pallas_call | solution.py:674
  2.9 99.2 %conditional.1 = ((bf16[256,1536]{1,0:T(8,128)(2,1)S(1)}, f32[16,8,128]{2,1,0:T(8,128)S(1)})) conditional(s32[]{:T(128)} %bitcast.1, (s32[2,12]{1,0:T(2,128)S(1)}, f32[3,12]{1,0:T(4,128)S(1)}, s32[1]{0:T(128)}, s32[1]{0:T(128)}, bf16[256,1536]{1,0:T(8,128)(2,1)}, /*index=5*/bf16[16,1536]{1,0:T(8,128)(2,1)}, ...), branch_computations={%region_0.0_spmd, %region_1.0_spmd, %region_2.0_spmd, %region_3.0_... | conditional | bytes 8 | solution.py:706
  2.9 98.3 %branch_1_fun.1 = (bf16[256,1536]{1,0:T(8,128)(2,1)S(1)}, f32[16,8,128]{2,1,0:T(8,128)S(1)}) custom-call(s32[2,12]{1,0:T(2,128)S(1)} %get-tuple-element.211.meta, f32[3,12]{1,0:T(4,128)S(1)} %get-tuple-element.212.closed, s32[1]{0:T(128)} %get-tuple-element.213.time_ref, s32[1]{0:T(128)} %get-tuple-element.214.seed_ref, ...), custom_call_target="tpu_custom_call" | custom-call | tf_op jit(solution)/shard_map/cond/branch_1_fun/pallas_call | solution.py:577
  102.1 0.9 copy.30
  102.9 0.6 copy.31

commit v5 on v4

--- a/solution.py
+++ b/solution.py
@@ -379,9 +379,7 @@
     for s in map(jnp.int32, range(min(AHEAD, n_rows))):
         start_cross(s)
 
-    @pl.loop(0, heads)
-    def _(s):
-        in_range(s, 0, n_a, start_frames)
+    for s in map(jnp.int32, range(3)):
         in_range(s, n_rows, heads, start_frames)
 
     depth = clean_ref.shape[1]
@@ -463,6 +461,8 @@
     @pl.loop(0, heads + 8)
     def _(i):
         in_range(i + AHEAD, 0, n_rows, start_cross)
+        in_range(i, 0, n_a, start_frames)
+        in_range(i + 3, max(n_rows, 3), heads, start_frames)
         in_range(i - 8, 0, heads, finish)
         in_range(i, heads + 3, heads + 4, lambda i: text_grads())
         in_range(i - 6, 0, n_a, relay)

time: 104 us -> 110 us (1.058)
  Pallas kernels: 99.9 us -> 106 us
    pallas_call x1, Pallas kernels: 98.3 us -> 105 us  [attention(): pl.pallas_call(functools.partial(attention_kernel, n_a, n_b, heads, frame...]
where the time goes in v5:
time: 110 us
  Pallas kernels  106 us (96%)
  local copies, waits for them, and re-layouts  1.52 us (1%)
  between operations  1.3 us (1%)
    pallas_call x1, Pallas kernels, attention(): pl.pallas_call(functools.partial(attention_kernel, n_a, n_b, heads, frame...  105 us

profile of v5, /device:TPU:1, one launch (start us, length us, event | category | flops | bytes accessed | tf_op | source)
XLA Modules:
  0.0 109.7 jit_solution(18172961504205413206)
XLA Ops:
  0.6 1.6 %shard_map.149 = (s32[1]{0:T(128)}, s32[2,12]{1,0:T(2,128)S(1)}, f32[3,12]{1,0:T(4,128)S(1)}) custom-call(s32[3,12]{1,0:T(4,128)} %bitcast.55), custom_call_target="tpu_custom_call" | custom-call | tf_op jit(solution)/shard_map/pallas_call | solution.py:674
  2.9 105.3 %conditional.1 = ((bf16[256,1536]{1,0:T(8,128)(2,1)S(1)}, f32[16,8,128]{2,1,0:T(8,128)S(1)})) conditional(s32[]{:T(128)} %bitcast.1, (s32[2,12]{1,0:T(2,128)S(1)}, f32[3,12]{1,0:T(4,128)S(1)}, s32[1]{0:T(128)}, s32[1]{0:T(128)}, bf16[256,1536]{1,0:T(8,128)(2,1)}, /*index=5*/bf16[16,1536]{1,0:T(8,128)(2,1)}, ...), branch_computations={%region_0.0_spmd, %region_1.0_spmd, %region_2.0_spmd, %region_3.0_... | conditional | bytes 8 | solution.py:706
  3.1 104.7 %branch_3_fun.1 = (bf16[256,1536]{1,0:T(8,128)(2,1)S(1)}, f32[16,8,128]{2,1,0:T(8,128)S(1)}) custom-call(s32[2,12]{1,0:T(2,128)S(1)} %get-tuple-element.245.meta, f32[3,12]{1,0:T(4,128)S(1)} %get-tuple-element.246.closed, s32[1]{0:T(128)} %get-tuple-element.247.time_ref, s32[1]{0:T(128)} %get-tuple-element.248.seed_ref, ...), custom_call_target="tpu_custom_call" | custom-call | tf_op jit(solution)/shard_map/cond/branch_3_fun/pallas_call | solution.py:577
  108.2 0.9 copy.30
  109.1 0.6 copy.31
